TPU v7x, 32 devices: a whole 2x2x4 slice. The times are simulated.
32 devices in a mesh: row: 4 (over y, x), col: 8 (over z, core).
Axes of the slice: x: 2, y: 2, z: 4, core: 2. Of those that a mesh axis runs over, the one named last changes fastest.
Arguments:
- kernel: float32 [10240, 10240], P('row', 'col'), may hold values from 0 to 3, as said below
- noise: float32 [10240], P('row'), may hold values from 0.3 to 1
Outputs:
- factored: float32 [10240, 10240], P('row', 'col')
Inputs may be any that keep to these rules, and one draw needn't show every extreme that they name: In global order kernel is symmetric and positive semidefinite, and all its entries are positive.
All inputs are finite; a program needn't handle non-finite values.
Results may differ from a plain program's by a relative error of at most 0.0001.
Values sent between devices are 32-bit elements; how exact they have to be, the bound alone decides.
No kernel may reach another device: no remote copies, remote signals or barrier semaphores. Data moves between devices by JAX's collectives and lax.ppermute only.
A program may use at most 128 MiB of HBM per device.

v0:
```python
import jax
import jax.numpy as jnp
from jax import lax
from jax.sharding import PartitionSpec as P

NB = 256


def broadcast(block, axis, source):
    block = jnp.where(lax.axis_index(axis) == source, block, jnp.zeros_like(block))
    return lax.psum(block, axis)


def factor_block(block):
    whole = jnp.tril(block) + jnp.tril(block, -1).T
    factor = jnp.linalg.cholesky(whole)
    eye = jnp.eye(block.shape[0], dtype=block.dtype)
    inverse = lax.linalg.triangular_solve(factor, eye, left_side=True, lower=True)
    return (factor, inverse)


def solve_rows(rows_in, inverse):
    return jnp.dot(
        rows_in, inverse.T, precision=lax.Precision.HIGHEST, preferred_element_type=jnp.float32
    )


def pick_rows(row_rows, n_row, n_col, col_index, col_count):
    groups = n_col // n_row
    shaped = row_rows.reshape(col_count, groups, NB, NB)
    chosen = lax.dynamic_index_in_dim(shaped, col_index // n_row, 1, keepdims=False)
    return chosen.reshape(col_count * NB, NB)


def panel_data(k, slab, n_row, n_col, col_index, col_count):
    diag_tile = broadcast(slab[:NB], "row", k % n_row)
    factor, inverse = factor_block(diag_tile)
    solved = solve_rows(slab, inverse)
    row_panel = broadcast(solved, "col", k)
    col_panel = broadcast(
        pick_rows(row_panel, n_row, n_col, col_index, col_count), "row", col_index % n_row
    )
    return (factor, row_panel, col_panel)


def advance(k, part, part_cols, row_block, col_index, row_panel, col_panel, factor):
    product = jnp.einsum(
        "rk,ck->rc",
        row_panel,
        col_panel,
        precision=lax.Precision.HIGHEST,
        preferred_element_type=jnp.float32,
    )
    touch = (row_block[:, None] >= part_cols[None, :]) & (part_cols[None, :] > k)
    part = jnp.where(touch, part - product, part)
    slab = part[:, :NB]
    owner = col_index == k
    slab = jnp.where((row_block > k)[:, None] & owner, row_panel, slab)
    factor_rows = jnp.tile(factor, (part.shape[0] // NB, 1))
    slab = jnp.where((row_block == k)[:, None] & owner, factor_rows, slab)
    part = jnp.concatenate([slab, part[:, NB:]], axis=1)
    return part


def body(kernel, noise):
    n_row = lax.axis_size("row")
    n_col = lax.axis_size("col")
    row_index = lax.axis_index("row")
    col_index = lax.axis_index("col")
    rows_local, cols_local = kernel.shape
    col_count = cols_local // NB
    row_iota = lax.iota(jnp.int32, rows_local)
    col_iota = lax.iota(jnp.int32, cols_local)
    row_block = row_iota // NB * n_row + row_index
    col_block = col_iota // NB * n_col + col_index
    row_elem = row_block * NB + row_iota % NB
    col_elem = col_block * NB + col_iota % NB
    matrix = kernel + jnp.where(row_elem[:, None] == col_elem[None, :], noise[:, None], 0.0)
    for k in range(2):
        factor, row_panel, col_panel = panel_data(
            k, matrix[:, :NB], n_row, n_col, col_index, col_count
        )
        matrix = advance(k, matrix, col_block, row_block, col_index, row_panel, col_panel, factor)
    return matrix


def solution(mesh):
    return jax.shard_map(
        body,
        mesh=mesh,
        in_specs=(P("row", "col"), P("row")),
        out_specs=P("row", "col"),
        check_vma=False,
    )
```

profile of v0, /device:TPU:0, one launch (start us, length us, event | category | flops | bytes accessed | tf_op | source)
XLA Modules:
  0.0 570.4 jit_solution(17009960013228196139)
XLA Ops:
  6.6 6.2 %select_add_fusion = f32[2560,1280]{1,0:T(8,128)S(1)} fusion(f32[2560,1280]{1,0:T(8,128)} %param.5, f32[2560]{0:T(1024)} %param.6, s32[1280]{0:T(1024)S(1)} %fusion.51, s32[2560]{0:T(1024)S(1)} %fusion.45), kind=kLoop, calls=%fused_computation.9 | loop fusion | flops 9830400 | bytes 26240000 | tf_op jit(solution)/shard_map/add | solution.py:78
  12.8 4.9 copy-done
  17.7 0.7 slice_select_fusion.3
  18.5 45.7 %all-reduce.8.cloned.1.call-done = f32[256,256]{1,0:T(8,128)} async-done(((f32[256,256]{1,0:T(8,128)}), f32[256,256]{1,0:T(8,128)}) %all-reduce.8.cloned.1.call-update) | async-done | bytes 262160 | tf_op jit(solution)/shard_map/psum | solution.py:11
  64.2 1.1 copy.3
  65.3 1.0 bitcast_add_fusion.3
  66.4 0.1 copy.5
  66.6 11.7 %cholesky.130 = f32[128,128]{1,0:T(8,128)S(1)} custom-call(f32[128,128]{1,0:T(8,128)S(1)} %cholesky.194), custom_call_target="Cholesky" | custom-call | tf_op jit(solution)/shard_map/jit(cholesky)/cholesky | solution.py:16
  78.3 9.8 %custom-call.13 = f32[1,128,128]{1,2,0:T(8,128)S(1)} custom-call(f32[1,128,128]{2,1,0:T(8,128)S(1)} %get-tuple-element.54), custom_call_target="InvertDiagBlocksLowerTriangular" | custom-call | tf_op jit(solution)/shard_map/jit(cholesky)/cholesky | solution.py:16
  88.2 0.2 constant_dynamic-update-slice_fusion.3
  88.4 0.3 convolution_subtract_fusion.3
  88.6 11.7 %cholesky.147 = f32[128,128]{1,0:T(8,128)S(1)} custom-call(f32[128,128]{1,0:T(8,128)S(1)} %convolution_subtract_fusion.3), custom_call_target="Cholesky" | custom-call | tf_op jit(solution)/shard_map/jit(cholesky)/cholesky | solution.py:16
  100.4 0.7 compare_reduce_fusion.2
  102.5 4.5 while.4
  103.0 0.6 fusion.73
  103.6 1.4 bitcast_dynamic-update-slice_fusion.4
  105.0 0.6 fusion.73
  105.6 1.4 bitcast_dynamic-update-slice_fusion.4
  107.0 19.7 %custom-call.14 = f32[2,128,128]{1,2,0:T(8,128)S(1)} custom-call(f32[2,128,128]{2,1,0:T(8,128)S(1)} %get-tuple-element.21), custom_call_target="InvertDiagBlocksLowerTriangular" | custom-call | tf_op jit(solution)/shard_map/triangular_solve/custom-call.0 | solution.py:18
  126.7 0.3 fusion.17
  127.0 0.3 convolution_subtract_fusion.1
  127.3 0.3 fusion.24
  127.6 5.5 convolution_select_fusion.1
  133.2 69.2 %all-reduce.10.cloned.1.call-done = f32[2560,256]{1,0:T(8,128)} async-done(((f32[2560,256]{1,0:T(8,128)}), f32[2560,256]{1,0:T(8,128)}) %all-reduce.10.cloned.1.call-update) | async-done | bytes 2621456 | tf_op jit(solution)/shard_map/psum | solution.py:11
  202.4 2.7 dynamic-slice_select_fusion.1
  205.2 56.1 %all-reduce.12.cloned.1.call-done = f32[1280,256]{1,0:T(8,128)} async-done(((f32[1280,256]{1,0:T(8,128)}), f32[1280,256]{1,0:T(8,128)}) %all-reduce.12.cloned.1.call-update) | async-done | bytes 1310736 | tf_op jit(solution)/shard_map/psum | solution.py:11
  261.3 17.0 %subtract_select_fusion.1 = f32[2560,1280]{1,0:T(8,128)S(1)} fusion(f32[2560,1280]{1,0:T(8,128)} %copy-done, f32[2560,256]{1,0:T(8,128)S(1)} %copy-done.3, f32[1280,256]{1,0:T(8,128)} %all-reduce.12.cloned.1.call-done, s32[1280]{0:T(1024)S(1)} %fusion.50, s32[2560]{0:T(1024)S(1)} %fusion.44, pred[1280]{0:T(1024)(128)(4,1)S(1)} %broadcast_compare_fusion), kind=kOutput, calls=%fused_computation.5 | convolution fusion | flops 10079436800 | bytes 30163200 | tf_op jit(solution)/shard_map/rk,ck->rc/dot_general | solution.py:47
  278.3 4.9 copy-done.1
  283.2 0.8 fusion.1
  284.0 0.8 slice_select_fusion.2
  284.9 0.2 all-reduce.16.cloned.1.call-start
  285.1 0.2 copy.7
  285.3 42.6 %all-reduce.14.cloned.1.call-done = f32[256,256]{1,0:T(8,128)} async-done(((f32[256,256]{1,0:T(8,128)}), f32[256,256]{1,0:T(8,128)}) %all-reduce.14.cloned.1.call-update) | async-done | bytes 262160 | tf_op jit(solution)/shard_map/psum | solution.py:11
  327.9 1.0 broadcast_select_fusion
  328.9 0.1 copy.8
  329.0 1.0 bitcast_add_fusion.1
  330.1 0.1 copy.9
  330.3 0.7 copy-done.6
  331.0 11.7 %cholesky.164 = f32[128,128]{1,0:T(8,128)S(1)} custom-call(f32[128,128]{1,0:T(8,128)S(1)} %cholesky.197), custom_call_target="Cholesky" | custom-call | tf_op jit(solution)/shard_map/jit(cholesky)/cholesky | solution.py:16
  342.7 9.8 %custom-call.15 = f32[1,128,128]{1,2,0:T(8,128)S(1)} custom-call(f32[1,128,128]{2,1,0:T(8,128)S(1)} %get-tuple-element.50), custom_call_target="InvertDiagBlocksLowerTriangular" | custom-call | tf_op jit(solution)/shard_map/jit(cholesky)/cholesky | solution.py:16
  352.6 1.0 constant_dynamic-update-slice_fusion.1
  353.6 1.1 convolution_subtract_fusion.2
  354.7 11.7 %cholesky.181 = f32[128,128]{1,0:T(8,128)S(1)} custom-call(f32[128,128]{1,0:T(8,128)S(1)} %convolution_subtract_fusion.2), custom_call_target="Cholesky" | custom-call | tf_op jit(solution)/shard_map/jit(cholesky)/cholesky | solution.py:16
  366.5 0.7 compare_reduce_fusion
  367.2 0.6 compare_reduce_fusion.1
  369.1 4.0 while.5
  369.3 0.6 fusion.74
  369.9 1.3 bitcast_dynamic-update-slice_fusion.5
  371.2 0.6 fusion.74
  371.8 1.3 bitcast_dynamic-update-slice_fusion.5
  373.1 0.6 copy-done.7
  373.7 20.5 %custom-call.16 = f32[2,128,128]{1,2,0:T(8,128)S(1)} custom-call(f32[2,128,128]{2,1,0:T(8,128)} %copy-done.7), custom_call_target="InvertDiagBlocksLowerTriangular" | custom-call | tf_op jit(solution)/shard_map/triangular_solve/custom-call.0 | solution.py:18
  394.2 0.3 fusion.15
  394.5 0.3 convolution_subtract_fusion
  394.8 0.3 fusion.20
  395.1 3.8 convolution_select_fusion
  398.9 69.2 %all-reduce.16.cloned.1.call-done = f32[2560,256]{1,0:T(8,128)} async-done(((f32[2560,256]{1,0:T(8,128)}), f32[2560,256]{1,0:T(8,128)}) %all-reduce.16.cloned.1.call-update) | async-done | bytes 2621456 | tf_op jit(solution)/shard_map/psum | solution.py:11
  468.1 2.5 dynamic-slice_select_fusion
  470.7 10.2 %slice.107 = f32[2560,1024]{1,0:T(8,128)} slice(f32[2560,1280]{1,0:T(8,128)} %copy-done.1), slice={[0:2560], [256:1280]} | slice | bytes 20971520 | tf_op jit(solution)/shard_map/slice | solution.py:61
  480.9 45.7 %all-reduce.18.cloned.1.call-done = f32[1280,256]{1,0:T(8,128)} async-done(((f32[1280,256]{1,0:T(8,128)}), f32[1280,256]{1,0:T(8,128)}) %all-reduce.18.cloned.1.call-update) | async-done | bytes 1310736 | tf_op jit(solution)/shard_map/psum | solution.py:11
  526.5 16.4 %subtract_select_fusion = f32[2560,1280]{1,0:T(8,128)S(1)} fusion(f32[2560,256]{1,0:T(8,128)} %all-reduce.16.cloned.1.call-done, f32[1280,256]{1,0:T(8,128)} %all-reduce.18.cloned.1.call-done, f32[2560,1024]{1,0:T(8,128)} %slice.107, f32[2560,256]{1,0:T(8,128)} %copy-done.2, s32[1280]{0:T(1024)S(1)} %copy-done.9, s32[2560]{0:T(1024)S(1)} %fusion.44, ...), kind=kOutput, calls=%fused_computation.4 | convolution fusion | flops 10082713600 | bytes 30163200 | tf_op jit(solution)/shard_map/rk,ck->rc/dot_general | solution.py:47
  542.9 5.6 slice.109
  548.6 4.0 fusion
  552.6 10.5 %pad_maximum_fusion = f32[2560,1280]{1,0:T(8,128)} fusion(f32[2560,1024]{1,0:T(8,128)} %slice.109, f32[2560,256]{1,0:T(8,128)} %fusion), kind=kLoop, calls=%fused_computation.8 | loop fusion | flops 3276800 | bytes 26214400 | tf_op jit(solution)/shard_map/concatenate | solution.py:61
  (58 shorter events, 0.9 us)
Async XLA Ops:
  6.5 57.7 %all-reduce.8.cloned.1.call-start = ((), (), s32[]{:S(2)}) async-start(), calls=%async_computation | async-start | bytes 524288 | tf_op jit(solution)/shard_map/psum | solution.py:11
  12.8 5.0 copy-start
  18.4 183.9 %all-reduce.10.cloned.1.call-start = ((), (), s32[]{:S(2)}) async-start(), calls=%async_computation.1 | async-start | bytes 5242880 | tf_op jit(solution)/shard_map/psum | solution.py:11
  133.1 128.2 %all-reduce.12.cloned.1.call-start = ((), (), s32[]{:S(2)}) async-start(), calls=%async_computation.2 | async-start | bytes 2621440 | tf_op jit(solution)/shard_map/psum | solution.py:11
  202.4 58.9 %copy-start.3 = (f32[2560,256]{1,0:T(8,128)S(1)}, f32[2560,256]{1,0:T(8,128)}, u32[]{:S(2)}) copy-start(f32[2560,256]{1,0:T(8,128)} %all-reduce.10.cloned.1.call-done) | copy-start | bytes 7864324
  205.1 122.9 %all-reduce.14.cloned.1.call-start = ((), (), s32[]{:S(2)}) async-start(), calls=%async_computation.3 | async-start | bytes 524288 | tf_op jit(solution)/shard_map/psum | solution.py:11
  205.2 73.1 %copy-start.8 = (s32[1280]{0:T(1024)}, s32[1280]{0:T(1024)S(1)}, u32[]{:S(2)}) copy-start(s32[1280]{0:T(1024)S(1)} %fusion.50) | copy-start | bytes 15364
  261.3 21.9 %copy-start.4 = (f32[2560,256]{1,0:T(8,128)S(1)}, f32[2560,256]{1,0:T(8,128)}, u32[]{:S(2)}) copy-start(f32[2560,256]{1,0:T(8,128)} %all-reduce.10.cloned.1.call-done) | copy-start | bytes 7864324
  278.2 5.0 copy-start.1
  284.0 111.1 %copy-start.2 = (f32[2560,256]{1,0:T(8,128)}, f32[2560,256]{1,0:T(8,128)S(1)}, u32[]{:S(2)}) copy-start(f32[2560,256]{1,0:T(8,128)S(1)} %fusion.1) | copy-start | bytes 7864324
  284.9 183.2 %all-reduce.16.cloned.1.call-start = ((), (), s32[]{:S(2)}) async-start(), calls=%async_computation.4 | async-start | bytes 5242880 | tf_op jit(solution)/shard_map/psum | solution.py:11
  330.3 0.7 copy-start.6
  366.5 2.6 copy-start.5
  373.1 0.6 copy-start.7
  398.9 127.6 %all-reduce.18.cloned.1.call-start = ((), (), s32[]{:S(2)}) async-start(), calls=%async_computation.5 | async-start | bytes 2621440 | tf_op jit(solution)/shard_map/psum | solution.py:11
  470.7 55.8 %copy-start.9 = (s32[1280]{0:T(1024)S(1)}, s32[1280]{0:T(1024)}, u32[]{:S(2)}) copy-start(s32[1280]{0:T(1024)} %copy-done.8) | copy-start | bytes 15364
Sparse Core Ops, SparseCore 0:
  18.6 45.6 all-reduce.7
  133.2 69.0 all-reduce.9
  205.7 55.4 all-reduce.11
  285.0 42.8 all-reduce.13
  399.0 69.0 all-reduce.15
  471.0 55.4 all-reduce.17
where the time goes:
time: 579 us; the launch traced here: 570 us
  waiting for transfers between devices  328 us (57%)
  other arithmetic  140 us (24%)
  matrix products  47 us (8%)
  local copies, waits for them, and re-layouts  36.4 us (6%)
  between operations  16.9 us (3%)
    psum x6, waiting for transfers between devices, broadcast(): return lax.psum(block, axis)  328 us
    another operation x13, other arithmetic, factor_block(): factor = jnp.linalg.cholesky(whole)  68.6 us
    another operation x5, other arithmetic, factor_block(): lax.linalg.triangular_solve(factor, eye, left_side=True, lower=True)  40.2 us
    dot_general x2, matrix products, advance(): jnp.einsum('rk,ck->rc', row_panel, col_panel, precision=lax.Precision.HIG...  33.4 us
    slice x2, local copies, waits for them, and re-layouts, advance(): part = jnp.concatenate([slab, part[:, NB:]], axis=1)  15.8 us
  transfers between devices with their start and end apart: 6, of which 6 were waited for; matrix products, arithmetic and copies ran while one was open for 2% of the time, Pallas kernels for 0%

commit v1 on v0

v1 whole, which is shorter than its diff:
```python
import functools
import jax
import jax.numpy as jnp
from jax import lax
from jax.sharding import PartitionSpec as P
from jax.experimental import pallas as pl
from jax.experimental.pallas import tpu as pltpu

NB = 256
HB = 128
HIGHEST = lax.Precision.HIGHEST


def dot_nt(a, b):
    return lax.dot_general(
        a, b, (((1,), (1,)), ((), ())), precision=HIGHEST, preferred_element_type=jnp.float32
    )


def dot_nn(a, b):
    return jnp.dot(a, b, precision=HIGHEST, preferred_element_type=jnp.float32)


def half_factor(work, unit, upper, lower_inv, spread):
    groups = HB // 8
    for b in range(groups):
        r0 = 8 * b
        cols = []
        for c in range(8):
            col = [
                jnp.broadcast_to(work[8 * g : 8 * g + 8, r0 + c : r0 + c + 1], (8, HB))
                for g in range(b, groups)
            ]
            spread[8 * c : 8 * c + 8, :] = col[0]
            cols.append(col)
        s = {}
        for c in range(8):
            for r in range(c, 8):
                s[r, c] = jnp.broadcast_to(spread[8 * c + r : 8 * c + r + 1, :], (8, HB))
        rows = [jnp.broadcast_to(work[r0 + r : r0 + r + 1, :], (8, HB)) for r in range(8)]
        unit_rows = [jnp.broadcast_to(unit[r0 + r : r0 + r + 1, :], (8, HB)) for r in range(8)]
        for k in range(8):
            scale = lax.rsqrt(s[k, k])
            for r in range(k + 1, 8):
                s[r, k] = s[r, k] * scale
            rows[k] = rows[k] * scale
            unit_rows[k] = unit_rows[k] * scale
            for g in range(1, groups - b):
                cols[k][g] = cols[k][g] * scale
            for c in range(k + 1, 8):
                for r in range(c, 8):
                    s[r, c] = s[r, c] - s[r, k] * s[c, k]
                rows[c] = rows[c] - s[c, k] * rows[k]
                unit_rows[c] = unit_rows[c] - s[c, k] * unit_rows[k]
                for g in range(1, groups - b):
                    cols[c][g] = cols[c][g] - s[c, k] * cols[k][g]
        for g in range(1, groups - b):
            at = slice(r0 + 8 * g, r0 + 8 * g + 8)
            take = [cols[k][g] * rows[k] for k in range(8)]
            work[at, :] = work[at, :] - (
                ((take[0] + take[1]) + (take[2] + take[3]))
                + ((take[4] + take[5]) + (take[6] + take[7]))
            )
            take = [cols[k][g] * unit_rows[k] for k in range(8)]
            unit[at, :] = unit[at, :] - (
                ((take[0] + take[1]) + (take[2] + take[3]))
                + ((take[4] + take[5]) + (take[6] + take[7]))
            )
        for k in range(8):
            upper[r0 + k : r0 + k + 1, :] = rows[k][:1]
            lower_inv[r0 + k : r0 + k + 1, :] = unit_rows[k][:1]


def first_half(block, work, unit, upper, lower_inv, spread, outs):
    factor, inverse, below, rest = outs
    row = lax.broadcasted_iota(jnp.int32, (HB, HB), 0)
    col = lax.broadcasted_iota(jnp.int32, (HB, HB), 1)
    work[...] = block[0]
    unit[...] = jnp.where(row == col, 1.0, 0.0)
    half_factor(work, unit, upper, lower_inv, spread)
    factor[...] = jnp.where(row >= col, upper[...].T, 0.0)
    inverse[...] = lower_inv[...]
    strip = dot_nt(block[1], lower_inv[...])
    below[...] = strip
    rest[...] = block[2] - dot_nt(strip, strip)


def start_kernel(block, factor, inverse, below, rest, work, unit, upper, lower_inv, spread):
    first_half(block, work, unit, upper, lower_inv, spread, (factor, inverse, below, rest))


def next_kernel(
    side, turned, block, prior, cross, factor, inverse, below, rest, left, work, unit, upper, lower_inv, spread
):
    raw = jnp.concatenate(
        [
            jnp.concatenate([side[0], turned[1].T], axis=1),
            jnp.concatenate([side[1], side[2]], axis=1),
        ],
        axis=0,
    )
    solved = dot_nt(raw, prior[...])
    cross[...] = solved
    update = dot_nt(solved, solved)
    left[0] = block[0] - update[:HB, :HB]
    left[1] = block[1] - update[HB:, :HB]
    left[2] = block[2] - update[HB:, HB:]
    first_half(left, work, unit, upper, lower_inv, spread, (factor, inverse, below, rest))


def finish_kernel(
    factor, inverse, below, rest, whole_factor, whole_inverse, work, unit, upper, lower_inv, spread
):
    row = lax.broadcasted_iota(jnp.int32, (HB, HB), 0)
    col = lax.broadcasted_iota(jnp.int32, (HB, HB), 1)
    work[...] = rest[...]
    unit[...] = jnp.where(row == col, 1.0, 0.0)
    half_factor(work, unit, upper, lower_inv, spread)
    whole_factor[:HB, :HB] = factor[...]
    whole_factor[:HB, HB:] = jnp.zeros((HB, HB), jnp.float32)
    whole_factor[HB:, :HB] = below[...]
    whole_factor[HB:, HB:] = jnp.where(row >= col, upper[...].T, 0.0)
    whole_inverse[:HB, :HB] = inverse[...]
    whole_inverse[:HB, HB:] = jnp.zeros((HB, HB), jnp.float32)
    whole_inverse[HB:, :HB] = -dot_nn(lower_inv[...], dot_nn(below[...], inverse[...]))
    whole_inverse[HB:, HB:] = lower_inv[...]


def factor_call(fn, args, outs, extra=()):
    half = pltpu.VMEM((HB, HB), jnp.float32)
    return pl.pallas_call(
        fn,
        out_shape=[jax.ShapeDtypeStruct(s, jnp.float32) for s in outs],
        scratch_shapes=[
            *extra,
            half,
            half,
            half,
            half,
            pltpu.VMEM((64, HB), jnp.float32),
        ],
        compiler_params=pltpu.CompilerParams(vmem_limit_bytes=32 * 2**20),
        cost_estimate=pl.CostEstimate(flops=0, bytes_accessed=0, transcendentals=0),
    )(*args)


QUARTERS = [(HB, HB)] * 4


def split(x):
    high = x.astype(jnp.bfloat16)
    return high, (x - high.astype(jnp.float32)).astype(jnp.bfloat16)


def mul(a, b):
    return jnp.dot(a, b, preferred_element_type=jnp.float32)


def mul_nt(a, b):
    return lax.dot_general(a, b, (((1,), (1,)), ((), ())), preferred_element_type=jnp.float32)


def wide_left(x):
    high, low = split(x)
    return jnp.concatenate([high, high, low], axis=1)


def wide_right(x):
    high, low = split(x)
    return jnp.concatenate([high, low, high], axis=1)


def solve_both(first, second, first_inverse, cross, second_inverse):
    left = mul_nt(wide_left(first), first_inverse)
    right = mul_nt(wide_left(second - mul_nt(wide_left(left), cross)), second_inverse)
    return left, right


def update_kernel(n_row, n_col, step_of, count, given, *refs):
    (place, matrix, noise, own, twin, here, there) = refs[:7]
    (first_factor, first_inverse, cross, second_factor, second_inverse) = refs[7:12]
    refs = refs[12:]
    if given is None:
        mine, other, out, high, low = refs[:5]
        refs = refs[5:]
    else:
        high, low, _, out = refs[:4]
        refs = refs[4:]
    tiles, rows_wide, edge, in_sem, out_sem = refs
    p, q = place[0], place[2]
    col_count = matrix.shape[1] // NB

    def rows_at(r):
        start = step_of(r) * NB
        return pl.ds(start if isinstance(start, int) else pl.multiple_of(start, NB), NB)

    def fetch(r):
        return pltpu.make_async_copy(matrix.at[rows_at(r), :], tiles.at[r], in_sem.at[r])

    def leave(r):
        return pltpu.make_async_copy(tiles.at[r], out.at[rows_at(r), :], out_sem.at[r])

    for r in range(count):
        fetch(r).start()
    inverses = (
        wide_right(first_inverse[...]),
        wide_right(cross[...]),
        wide_right(second_inverse[...]),
    )
    if given is None:
        odd = place[1] == 1
        left, right = solve_both(
            jnp.where(odd, other[...], mine[...]), jnp.where(odd, mine[...], other[...]), *inverses
        )
        high[:NB], low[:NB] = split(left.T)
        high[NB:], low[NB:] = split(right.T)
    by_columns = jnp.where(place[5] == 1, here[...], there[...])
    by_core = jnp.where(place[6] == 0, twin[...], own[...])
    first = jnp.where(place[3] == 1, own[...], twin[...])
    second = jnp.where(place[4] == 1, by_columns, by_core)
    left, right = solve_both(first.reshape(-1, NB), second.reshape(-1, NB), *inverses)
    edge[...] = jnp.where(q == 0, left, right).reshape(edge.shape)
    left_high, left_low = split(left)
    right_high, right_low = split(right)
    rows_wide[:, :NB] = left_high
    rows_wide[:, NB : 2 * NB] = right_high
    rows_wide[:, 2 * NB : 3 * NB] = left_low
    rows_wide[:, 3 * NB :] = right_low
    row = lax.broadcasted_iota(jnp.int32, (NB, NB), 0)
    col = lax.broadcasted_iota(jnp.int32, (NB, NB), 1)

    def one(r, _):
        here = pl.ds(pl.multiple_of(r * NB, NB), NB)
        i = step_of(r) * n_row + p
        active = jnp.minimum(lax.div(i - q + n_col, n_col), col_count)
        fetch(r).wait()
        for blocks in range(1, col_count + 1):

            @pl.when(active == blocks)
            def _():
                both = rows_wide[here, : 2 * NB]
                wide = jnp.concatenate([both, both, rows_wide[here, 2 * NB :]], axis=1)
                for c in range(blocks):
                    at = slice(c * NB, c * NB + NB)
                    tall = jnp.concatenate([high[:, at], low[:, at], high[:, at]], axis=0)
                    tiles[r, :, at] = tiles[r, :, at] - mul(wide, tall)

                @pl.when(i == (blocks - 1) * n_col + q)
                def _():
                    tiles[r, :, at] += jnp.where(row == col, noise[step_of(r)], 0.0)

        @pl.when((q < 2) & (i > q))
        def _():
            tiles[r, :, :NB] = jnp.where((q == 0) & (i == 1), cross[...], edge[r])

        @pl.when((q < 2) & (i == q))
        def _():
            tiles[r, :, :NB] = jnp.where(q == 0, first_factor[...], second_factor[...])

        leave(r).start()
        return 0

    lax.fori_loop(0, count, one, 0)
    for r in range(count):
        leave(r).wait()


def update(place, step_of, count, matrix, noise, rows, factored, n_row, n_col, cols=None, done=None):
    cols_local = matrix.shape[1]
    whole = pl.BlockSpec(memory_space=pltpu.VMEM)
    anywhere = pl.BlockSpec(memory_space=pl.ANY)
    part = jax.ShapeDtypeStruct((2 * NB, cols_local), jnp.bfloat16)
    result = jax.ShapeDtypeStruct(matrix.shape, jnp.float32)
    extra = cols if done is None else (*done[1:], done[0])
    solved = count + (cols_local // NB if done is None else 0)
    flops = 2 * 3 * NB * NB * (solved * 3 * NB + count * cols_local)
    outs = pl.pallas_call(
        functools.partial(update_kernel, n_row, n_col, step_of, count, done),
        in_specs=[pl.BlockSpec(memory_space=pltpu.SMEM), anywhere]
        + [whole] * 10
        + ([whole, whole] if done is None else [whole, whole, anywhere]),
        out_specs=[anywhere, whole, whole] if done is None else anywhere,
        out_shape=[result, part, part] if done is None else result,
        scratch_shapes=[
            pltpu.VMEM((count, NB, cols_local), jnp.float32),
            pltpu.VMEM((count * NB, 4 * NB), jnp.bfloat16),
            pltpu.VMEM((count, NB, NB), jnp.float32),
            pltpu.SemaphoreType.DMA((count,)),
            pltpu.SemaphoreType.DMA((count,)),
        ],
        input_output_aliases={} if done is None else {14: 0},
        compiler_params=pltpu.CompilerParams(vmem_limit_bytes=40 * 2**20),
        cost_estimate=pl.CostEstimate(
            flops=flops, bytes_accessed=count * NB * cols_local * 8, transcendentals=0
        ),
    )(place, matrix, noise, *rows, *factored, *extra)
    return outs if done is None else (outs, *done[1:])


def start_factor(corner):
    return factor_call(start_kernel, [corner], QUARTERS)


def finish_factor(part, side, turned, next_corner, before_first=(), before_last=()):
    part = [after(part[0], *before_first), *part[1:]]
    first_factor, first_inverse = factor_call(finish_kernel, part, [(NB, NB)] * 2)
    cross, *part = factor_call(
        next_kernel,
        [side, turned, next_corner, first_inverse],
        [(NB, NB)] + QUARTERS,
        [pltpu.VMEM((3, HB, HB), jnp.float32)],
    )
    part = [after(part[0], *before_last), *part[1:]]
    second_factor, second_inverse = factor_call(finish_kernel, part, [(NB, NB)] * 2)
    return first_factor, first_inverse, cross, second_factor, second_inverse


def low_part(x):
    return jnp.stack([x[:HB, :HB], x[HB:, :HB], x[HB:, HB:]])


def after(x, *others):
    return lax.optimization_barrier((x, *others))[0]


def blocks_of(x):
    return x.reshape(-1, NB, NB)


def head_noise(noise):
    return jnp.where(jnp.arange(NB)[:, None] == jnp.arange(NB)[None, :], noise[:NB, None], 0.0)


def arrange(own, other, core):
    first = jnp.where(core == 0, own, other)
    second = jnp.where(core == 0, other, own)
    return first[0], first[1], second[0], second[1]


def body_general(kernel, noise):
    n_row = lax.axis_size("row")
    n_col = lax.axis_size("col")
    p = lax.axis_index("row")
    q = lax.axis_index("col")
    chunks = kernel.shape[0] // NB
    planes = n_col // 2
    plane = q // 2
    core = q % 2

    def twin(x):
        return lax.ppermute(x, "col", [(c, c ^ 1) for c in range(n_col)])

    mine = blocks_of(kernel[:, :NB])
    sent, other, got = [], [], None
    for s in range(chunks + planes - 1):
        now = mine[0] if s == 0 else got
        if 0 < s < chunks:
            now = jnp.where(plane == 0, mine[s], got)
        sent.append(now)
        other.append(twin(now))
        pairs = [
            (2 * z + c, 2 * z + 2 + c)
            for z in range(planes - 1)
            if 0 <= s - z < chunks
            for c in range(2)
        ]
        if pairs:
            got = lax.ppermute(now, "col", pairs)
    own = lax.dynamic_slice_in_dim(jnp.stack(sent), plane, chunks)
    other = lax.dynamic_slice_in_dim(jnp.stack(other), plane, chunks)

    block = own[0]
    block = low_part(jnp.where(p == core, block + head_noise(noise), block))
    swapped = lax.ppermute(block, "row", [(r, r ^ 1) for r in range(2)])
    even = p % 2 == 0
    strip = jnp.stack([jnp.where(even, block, swapped), jnp.where(even, swapped, block)])
    step = 2
    while step < n_row:
        more = lax.ppermute(strip, "row", [(r, r + step) for r in range(step)])
        strip = jnp.where(p >= step, more, strip)
        step *= 2
    corner, *rest = arrange(strip, twin(strip), core)
    factored = finish_factor(start_factor(corner), *rest)

    tops = lax.all_gather(kernel[:NB].T, "row")
    none = jnp.zeros_like(p)
    place = jnp.stack([p, none, q, 1 - core, none, none, core]).astype(jnp.int32)
    return update(
        place,
        lambda r: r,
        chunks,
        kernel,
        noise.reshape(-1, 1, NB),
        (own, other, own, own),
        factored,
        n_row,
        n_col,
        cols=(tops[0], tops[1]),
    )[0]


BOTH = ("row", "col")
N_COL = 8


def route(x, pairs):
    return lax.ppermute(x, BOTH, [(a[0] * N_COL + a[1], b[0] * N_COL + b[1]) for a, b in pairs])


def spread_inverses(factored, earlier, between, plane, core):
    _, first, cross, _, second = factored
    halves = (
        jnp.concatenate([low_part(first), jnp.stack([cross[:HB, :HB], cross[:HB, HB:]])]),
        jnp.concatenate([jnp.stack([cross[HB:, :HB], cross[HB:, HB:]]), low_part(second)]),
    )
    here = after(jnp.where(core == 0, halves[0], halves[1]), *earlier)
    z = route(here, [((r, c), (r, 4 + c)) for r in range(4) for c in (0, 1)])
    here = after(jnp.where(plane == 2, z, here), *between)
    z = route(here, [((r, k + c), (r, k + 2 + c)) for r in range(4) for k in (0, 4) for c in (0, 1)])
    here = jnp.where(plane % 2 == 1, z, here)
    other = route(here, TWINS)
    top = jnp.where(core == 0, here, other)
    low = jnp.where(core == 0, other, here)
    zero = jnp.zeros((HB, HB), jnp.float32)

    def square(a, b, c, d):
        return jnp.concatenate(
            [jnp.concatenate([a, b], axis=1), jnp.concatenate([c, d], axis=1)], axis=0
        )

    return (
        square(top[0], zero, top[1], top[2]),
        square(top[3], top[4], low[0], low[1]),
        square(low[2], zero, low[3], low[4]),
    )


TWINS = [((r, c), (r, c ^ 1)) for r in range(4) for c in range(N_COL)]


def body_four(kernel, noise):
    p = lax.axis_index("row")
    q = lax.axis_index("col")
    plane = q // 2
    core = q % 2
    home = core == p % 2
    low_line = p < 2
    n_cols = kernel.shape[1] // NB
    cut = (n_cols - 1) // 2
    early, late = slice(1, 1 + cut), slice(1 + cut, 1 + 2 * cut)

    strips = kernel.reshape(n_cols, 2, NB, -1)

    def even(part):
        return strips[part, 0, :, :NB]

    def odd(part):
        return strips[part, 1, :, :NB]

    blocks = blocks_of(kernel[:NB].T)
    middle = blocks[early]
    others = jnp.concatenate([blocks[:1], blocks[late]], axis=0)
    along_y = [((a, c), (a + 2, c)) for a in range(2) for c in range(N_COL)]
    along_x = [((a, c), (a ^ 1, c)) for a in range(4) for c in range(N_COL)]
    low, high = (0, 1), (2, 3)
    up = lambda z, lines: [((r, 2 * z + c), (r, 2 * z + 2 + c)) for r in lines for c in (0, 1)]
    lift = [((s, 4 + r), (r, 6 + s)) for r in low for s in (0, 1)]
    side = [((2 + s, r), (r, 4 + s)) for r in high for s in (0, 1)]
    corner = kernel[:NB, :NB]
    corner = low_part(jnp.where(p == core, corner + head_noise(noise), corner))

    got = route(corner, [((r, c), (r + 2, c)) for r in (0, 1) for c in (0, 1)])
    y1 = route(after(middle, got), along_y)
    h1 = route(jnp.where(plane == 0, even(early), middle), up(0, low) + lift)
    here = jnp.where(low_line, corner, got)
    lead_x = route(here, [((r, c), (r ^ 1, c)) for r in range(4) for c in (0, 1)])
    is_even = p % 2 == 0
    lead = jnp.stack([jnp.where(is_even, here, lead_x), jnp.where(is_even, lead_x, here)])
    lead_twin = route(lead, [((r, c), (r, c ^ 1)) for r in range(4) for c in (0, 1)])
    corner, *rest = arrange(lead, lead_twin, core)
    begun = start_factor(after(corner, h1))

    others = after(others, lead_x)
    y2 = route(others, along_y)
    mine1 = jnp.where(low_line, after(middle, lead_x), y1)
    x1 = route(after(mine1, begun[0]), along_x)

    h2 = route(
        jnp.where(
            plane == 0,
            even(late),
            jnp.where(plane == 1, jnp.where(low_line, h1, mine1), others[1:]),
        ),
        up(0, low) + up(1, low) + side + lift,
    )
    down = [((s, 4 + r), (r, 2 + s)) for r in low for s in (0, 1)]
    down += [((2 + s, 4 + r), (r, 4 + s)) for r in high for s in (0, 1)]
    d1 = route(after(mine1, begun[0]), down)
    e1 = route(odd(slice(0, n_cols)), up(0, high))
    factored = finish_factor(begun, *rest, before_last=(x1, h2, y2, d1, e1))
    mine2 = jnp.where(low_line, after(others, factored[2]), y2)
    x2 = route(after(mine2, x1), along_x)
    d2 = route(mine2, down)
    h2 = after(h2, factored[2])
    h3 = route(
        jnp.where((plane == 1) & ~low_line, mine2[1:], h2), up(1, low) + side + up(2, low + high)
    )
    h4 = route(h3, up(2, low + high))
    inverses = spread_inverses(factored, (h2,), (x2,), plane, core)
    factored = (factored[0], inverses[0], inverses[1], factored[3], inverses[2])

    given = lambda x, y: jnp.concatenate([y[:1], x, y[1:]], axis=0)
    col_mine = given(mine1, mine2)
    col_given = given(x1, x2)
    first_cols = jnp.where(is_even, col_mine, col_given)
    second_cols = jnp.where(is_even, col_given, col_mine)
    homes = [((r, c), (r, c ^ 1)) for r, c in [(0, 4), (1, 5), (2, 6), (3, 7), (2, 2), (3, 3)]]
    second_twin = route(second_cols, homes)

    by_odd = (low_line & (plane == 2)) | (~low_line & (plane == 3))
    by_even = ~low_line & (plane == 1)
    own_1 = jnp.where(
        by_odd,
        first_cols,
        jnp.where(
            plane == 0,
            odd(slice(0, n_cols)),
            jnp.where(
                by_even,
                e1,
                jnp.where(plane == 3, jnp.concatenate([h1[:1], h1, h2], axis=0), given(d1, d2)),
            ),
        ),
    )
    own_2 = jnp.where(
        plane == 0,
        even(slice(0, 1 + cut)),
        jnp.where(
            by_even,
            first_cols[: 1 + cut],
            given(jnp.where(plane == 1, h1, jnp.where(plane == 2, h2, h3)), h1[:1]),
        ),
    )

    def rows(own, part):
        return own, route(own, TWINS), second_cols[part], second_twin[part]

    def place(by):
        flags = [p, p % 2, q, jnp.where(by, home, core == 0), by, home, core]
        return jnp.stack([x.astype(jnp.int32) for x in flags])

    noise_rows = noise.reshape(-1, 1, NB)
    rows_1 = rows(own_1, slice(0, n_cols))
    rows_2 = rows(own_2, slice(0, 1 + cut))
    cols = (col_mine.reshape(-1, NB), col_given.reshape(-1, NB))
    done = update(
        place(by_odd),
        lambda r: 2 * r + 1,
        n_cols,
        kernel,
        noise_rows,
        rows_1,
        factored,
        4,
        N_COL,
        cols=cols,
    )
    h4 = after(h4, done[1])
    own_3 = jnp.where(
        plane == 0,
        even(late),
        jnp.where(
            by_even,
            first_cols[late],
            jnp.where(plane == 1, h2, jnp.where(plane == 2, h3, h4)),
        ),
    )
    rows_3 = rows(own_3, late)
    done = update(
        place(by_even), lambda r: 2 * r, 1 + cut, kernel, noise_rows, rows_2, factored, 4, N_COL, done=done
    )
    return update(
        place(by_even),
        lambda r: 2 * (1 + cut + r),
        cut,
        kernel,
        noise_rows,
        rows_3,
        factored,
        4,
        N_COL,
        done=done,
    )[0]


def body(kernel, noise):
    rows, cols = kernel.shape[0] // NB, kernel.shape[1] // NB
    mesh_of_four = lax.axis_size("row") == 4 and lax.axis_size("col") == N_COL
    if mesh_of_four and rows == 2 * cols and cols % 2 == 1 and cols > 2:
        return body_four(kernel, noise)
    return body_general(kernel, noise)


def solution(mesh):
    return jax.shard_map(
        body,
        mesh=mesh,
        in_specs=(P("row", "col"), P("row")),
        out_specs=P("row", "col"),
        check_vma=False,
    )
```

time: 579 us -> 141 us (0.24); the launches traced: 570 us -> 139 us
  waiting for transfers between devices: 328 us -> 10.4 us
  other arithmetic: 140 us -> 17.3 us
  starting transfers between devices: 0.38 us -> 55.4 us
  matrix products: 47 us -> 0 us
  Pallas kernels: 0 us -> 42.2 us
  local copies, waits for them, and re-layouts: 36.4 us -> 13 us
  between operations: 16.9 us -> 1.06 us
    psum x6 -> x0, waiting for transfers between devices: 328 us -> none  [broadcast(): return lax.psum(block, axis)]
    another operation x18 -> x3, other arithmetic: 109 us -> 1.71 us  [the longest x2 1.01 us: body_four(): jnp.stack([jnp.where(is_even, here, lead_x), jnp.where(is_even, lead_x, h...]
    ppermute x0 -> x21, starting transfers between devices: none -> 55.4 us  [route(): lax.ppermute(x, BOTH, [(a[0] * N_COL + a[1], b[0] * N_COL + b[1]) for a,...]
    dot_general x4 -> x0, matrix products: 42.7 us -> none  [the longest x2 33.4 us: advance(): jnp.einsum('rk,ck->rc', row_panel, col_panel, precision=lax.Precision.HIG...]
    pallas_call x0 -> x7, Pallas kernels: none -> 42.2 us  [the longest x3 25.3 us: update(): pl.pallas_call(functools.partial(update_kernel, n_row, n_col, step_of, co...]
    ppermute x0 -> x21, waiting for transfers between devices: none -> 10.4 us  [route(): lax.ppermute(x, BOTH, [(a[0] * N_COL + a[1], b[0] * N_COL + b[1]) for a,...]
    slice x2 -> x17, local copies, waits for them, and re-layouts: 15.8 us -> 6.67 us  [the longest x4 2.5 us: rows(): return (own, route(own, TWINS), second_cols[part], second_twin[part])]
    concatenate x1 -> x5, other arithmetic: 10.5 us -> 2.05 us  [the longest x1 1.92 us: body_four(): given = lambda x, y: jnp.concatenate([y[:1], x, y[1:]], axis=0)]
  transfers between devices with their start and end apart: 6 -> 21, of which waited for: 6 -> 4; matrix products, arithmetic and copies ran while one was open for 2% -> 14% of each run, Pallas kernels for 0% -> 26%
where the time goes in v1:
time: 141 us; the launch traced here: 139 us
  starting transfers between devices  55.4 us (39%)
  Pallas kernels  42.2 us (30%)
  other arithmetic  17.3 us (12%)
  local copies, waits for them, and re-layouts  13 us (9%)
  waiting for transfers between devices  10.4 us (7%)
    ppermute x21, starting transfers between devices, route(): lax.ppermute(x, BOTH, [(a[0] * N_COL + a[1], b[0] * N_COL + b[1]) for a,...  55.4 us
    pallas_call x3, Pallas kernels, update(): pl.pallas_call(functools.partial(update_kernel, n_row, n_col, step_of, co...  25.3 us
    pallas_call x4, Pallas kernels, factor_call(): pl.pallas_call(fn, out_shape=[jax.ShapeDtypeStruct(s, jnp.float32) for s...  16.9 us
    ppermute x21, waiting for transfers between devices, route(): lax.ppermute(x, BOTH, [(a[0] * N_COL + a[1], b[0] * N_COL + b[1]) for a,...  10.4 us
    select_n x1, other arithmetic, body_four(): jnp.where(plane == 1, h1, jnp.where(plane == 2, h2, h3))  3.7 us
    unnamed x70, local copies, waits for them, and re-layouts  3.47 us
    select_n x1, other arithmetic, body_four(): jnp.where(by_odd, first_cols, jnp.where(plane == 0, odd(slice(0, n_cols))...  3.08 us
  transfers between devices with their start and end apart: 21, of which 4 were waited for; matrix products, arithmetic and copies ran while one was open for 14% of the time, Pallas kernels for 26%

profile of v1, /device:TPU:0, one launch (start us, length us, event | category | flops | bytes accessed | tf_op | source)
XLA Modules:
  0.0 139.3 jit_solution(11725404540050388284)
XLA Ops:
  0.0 0.7 slice.173
  0.7 1.0 add_select_fusion
  1.8 0.7 pad_maximum_fusion.4
  2.5 4.9 %collective-permute-start = (f32[3,128,128]{2,1,0:T(8,128)}, f32[3,128,128]{2,1,0:T(8,128)S(1)}, u32[]{:S(2)}, u32[]{:S(2)}) collective-permute-start(f32[3,128,128]{2,1,0:T(8,128)} %pad_maximum_fusion.4), channel_id=1, source_target_pairs={{0,16},{1,17},{8,24},{9,25}} | collective-permute-start | bytes 589832 | tf_op jit(solution)/shard_map/ppermute | solution.py:407
  7.4 0.0 slice-start.4
  7.4 1.3 slice-done.4
  8.7 0.4 copy.12
  9.1 0.1 fusion.6
  9.2 1.9 %fusion.5 = f32[2,256,256]{2,1,0:T(8,128)} fusion(f32[2,256,256]{2,1,0:T(8,128)S(1)} %bitcast.113, f32[5,2,256,1280]{3,2,1,0:T(8,128)} %bitcast.103, pred[]{:T(512)S(6)} %eq.35), kind=kLoop, calls=%fused_computation.16 | loop fusion | flops 131072 | bytes 1572865 | tf_op jit(solution)/shard_map/jit(_where)/select_n | solution.py:474
  11.1 1.3 collective-permute-start.3
  12.4 2.5 %slice_bitcast_fusion = f32[5,256,256]{2,1,0:T(8,128)} fusion(f32[5,2,256,1280]{3,2,1,0:T(8,128)} %bitcast.104), kind=kLoop, calls=%fused_computation | loop fusion | bytes 2621440 | tf_op jit(solution)/shard_map/squeeze | solution.py:458
  15.0 1.7 %collective-permute-start.11 = (f32[5,256,256]{2,1,0:T(8,128)}, f32[5,256,256]{2,1,0:T(8,128)}, u32[]{:S(2)}, u32[]{:S(2)}) collective-permute-start(f32[5,256,256]{2,1,0:T(8,128)} %slice_bitcast_fusion), channel_id=1, source_target_pairs={{16,18},{17,19},{24,26},{25,27}} | collective-permute-start | bytes 3932168 | tf_op jit(solution)/shard_map/ppermute | solution.py:407
  16.7 3.4 %collective-permute-start.1 = (f32[3,128,128]{2,1,0:T(8,128)S(1)}, f32[3,128,128]{2,1,0:T(8,128)}, u32[]{:S(2)}, u32[]{:S(2)}) collective-permute-start(f32[3,128,128]{2,1,0:T(8,128)S(1)} %broadcast_select_fusion.12), channel_id=1, source_target_pairs={{0,8},{1,9},{8,0},{9,1},{16,24},{17,25},{24,16},{25,17}} | collective-permute-start | bytes 589832 | tf_op jit(solution)/shard_map/ppermute | solution.py:407
  20.1 3.7 %collective-permute-start.5 = (f32[2,256,256]{2,1,0:T(8,128)S(1)}, f32[2,256,256]{2,1,0:T(8,128)}, u32[]{:S(2)}, u32[]{:S(2)}) collective-permute-start(f32[2,256,256]{2,1,0:T(8,128)S(1)} %bitcast.114), channel_id=1, source_target_pairs={{0,16},{1,17},{2,18},{3,19},{4,20},{5,21},{6,22},{7,23},{8,24},{9,... | collective-permute-start | bytes 1572872 | tf_op jit(solution)/shard_map/ppermute | solution.py:407
  23.9 1.2 collective-permute-done.1
  25.1 1.0 select_bitcast_fusion.1
  26.1 1.9 %collective-permute-start.2 = (f32[2,3,128,128]{3,2,1,0:T(8,128)S(1)}, f32[2,3,128,128]{3,2,1,0:T(8,128)S(1)}, u32[]{:S(2)}, u32[]{:S(2)}) collective-permute-start(f32[2,3,128,128]{3,2,1,0:T(8,128)S(1)} %pad_maximum_fusion.3), channel_id=1, source_target_pairs={{0,1},{1,0},{8,9},{9,8},{16,17},{17,16},{24,25},{25,24}} | collective-permute-start | bytes 1179656 | tf_op jit(solution)/shard_map/ppermute | solution.py:407
  28.0 0.1 pad_maximum_fusion.2
  28.1 3.0 %collective-permute-start.4 = (f32[3,256,256]{2,1,0:T(8,128)S(1)}, f32[3,256,256]{2,1,0:T(8,128)S(1)}, u32[]{:S(2)}, u32[]{:S(2)}) collective-permute-start(f32[3,256,256]{2,1,0:T(8,128)S(1)} %pad_maximum_fusion.2), channel_id=1, source_target_pairs={{0,16},{1,17},{2,18},{3,19},{4,20},{5,21},{6,22},{7,23},{8,24},{9,... | collective-permute-start | bytes 2359304 | tf_op jit(solution)/shard_map/ppermute | solution.py:407
  31.1 4.2 %collective-permute-done.5 = f32[2,256,256]{2,1,0:T(8,128)} collective-permute-done((f32[2,256,256]{2,1,0:T(8,128)S(1)}, f32[2,256,256]{2,1,0:T(8,128)}, u32[]{:S(2)}, u32[]{:S(2)}) %collective-permute-start.5) | collective-permute-done | bytes 524320 | tf_op jit(solution)/shard_map/ppermute | solution.py:407
  35.4 1.2 select_select_fusion.1
  36.6 1.3 collective-permute-start.8
  38.0 0.1 broadcast_select_fusion.5
  38.1 4.1 %shard_map.28 = (f32[128,128]{1,0:T(8,128)S(1)}, f32[128,128]{1,0:T(8,128)S(1)}, f32[128,128]{1,0:T(8,128)S(1)}, f32[128,128]{1,0:T(8,128)S(1)}) custom-call(f32[3,128,128]{2,1,0:T(8,128)S(1)} %get-tuple-element.34.block), custom_call_target="tpu_custom_call" | custom-call | tf_op jit(solution)/shard_map/pallas_call | solution.py:131
  42.1 0.9 collective-permute-start.13
  43.0 0.1 collective-permute-start.6
  43.1 3.8 %shard_map.29 = (f32[256,256]{1,0:T(8,128)S(1)}, f32[256,256]{1,0:T(8,128)S(1)}) custom-call(f32[128,128]{1,0:T(8,128)S(1)} %get-tuple-element.35.factor, f32[128,128]{1,0:T(8,128)S(1)} %get-tuple-element.36.inverse, f32[128,128]{1,0:T(8,128)S(1)} %get-tuple-element.37.below, f32[128,128]{1,0:T(8,128)S(1)} %get-tuple-element.38.rest), custom_call_target="tpu_custom_call" | custom-call | tf_op jit(solution)/shard_map/pallas_call | solution.py:131
  47.0 0.7 copy-done.6
  47.7 5.2 %shard_map.30 = (f32[256,256]{1,0:T(8,128)S(1)}, f32[128,128]{1,0:T(8,128)S(1)}, f32[128,128]{1,0:T(8,128)S(1)}, f32[128,128]{1,0:T(8,128)S(1)}, f32[128,128]{1,0:T(8,128)S(1)}) custom-call(f32[3,128,128]{2,1,0:T(8,128)S(1)} %get-tuple-element.79.side, f32[3,128,128]{2,1,0:T(8,128)S(1)} %get-tuple-element.81.turned, ...), custom_call_target="tpu_custom_call" | custom-call | tf_op jit(solution)/shard_map/pallas_call | solution.py:131
  52.9 0.1 broadcast_select_fusion.2
  53.0 0.7 collective-permute-start.12
  53.8 2.1 %collective-permute-start.7 = (f32[3,256,256]{2,1,0:T(8,128)S(1)}, f32[3,256,256]{2,1,0:T(8,128)}, u32[]{:S(2)}, u32[]{:S(2)}) collective-permute-start(f32[3,256,256]{2,1,0:T(8,128)S(1)} %broadcast_select_fusion.2), channel_id=1, source_target_pairs={{0,8},{1,9},{2,10},{3,11},{4,12},{5,13},{6,14},{7,15},{8,0},{9,1},... | collective-permute-start | bytes 2359304 | tf_op jit(solution)/shard_map/ppermute | solution.py:407
  55.9 3.8 %shard_map.31 = (f32[256,256]{1,0:T(8,128)S(1)}, f32[256,256]{1,0:T(8,128)S(1)}) custom-call(f32[128,128]{1,0:T(8,128)S(1)} %get-tuple-element.49.factor, f32[128,128]{1,0:T(8,128)S(1)} %get-tuple-element.50.inverse, f32[128,128]{1,0:T(8,128)S(1)} %get-tuple-element.51.below, f32[128,128]{1,0:T(8,128)S(1)} %get-tuple-element.52.rest), custom_call_target="tpu_custom_call" | custom-call | tf_op jit(solution)/shard_map/pallas_call | solution.py:131
  59.7 0.7 copy-done.9
  60.5 6.5 %collective-permute-start.16 = (f32[5,128,128]{2,1,0:T(8,128)S(1)}, f32[5,128,128]{2,1,0:T(8,128)}, u32[]{:S(2)}, u32[]{:S(2)}) collective-permute-start(f32[5,128,128]{2,1,0:T(8,128)S(1)} %broadcast_select_fusion.11), channel_id=1, source_target_pairs={{0,4},{1,5},{8,12},{9,13},{16,20},{17,21},{24,28},{25,29}} | collective-permute-start | bytes 983048 | tf_op jit(solution)/shard_map/ppermute | solution.py:407
  67.1 0.9 broadcast_select_fusion.4
  68.0 1.4 %collective-permute-start.9 = (f32[2,256,256]{2,1,0:T(8,128)}, f32[2,256,256]{2,1,0:T(8,128)}, u32[]{:S(2)}, u32[]{:S(2)}) collective-permute-start(f32[2,256,256]{2,1,0:T(8,128)} %get-tuple-element.72), channel_id=1, source_target_pairs={{2,4},{3,5},{10,12},{11,13},{18,20},{26,21},{19,28},{27,29},{4,6},... | collective-permute-start | bytes 1572872 | tf_op jit(solution)/shard_map/ppermute | solution.py:407
  69.5 3.5 %collective-permute-done.16 = f32[5,128,128]{2,1,0:T(8,128)} collective-permute-done((f32[5,128,128]{2,1,0:T(8,128)S(1)}, f32[5,128,128]{2,1,0:T(8,128)}, u32[]{:S(2)}, u32[]{:S(2)}) %collective-permute-start.16) | collective-permute-done | bytes 327712 | tf_op jit(solution)/shard_map/ppermute | solution.py:407
  73.0 18.0 %collective-permute-start.17 = (f32[5,128,128]{2,1,0:T(8,128)S(1)}, f32[5,128,128]{2,1,0:T(8,128)S(1)}, u32[]{:S(2)}, u32[]{:S(2)}) collective-permute-start(f32[5,128,128]{2,1,0:T(8,128)S(1)} %broadcast_select_fusion.7), channel_id=1, source_target_pairs={{0,2},{1,3},{4,6},{5,7},{8,10},{9,11},{12,14},{13,15},{16,18},{17,... | collective-permute-start | bytes 983048 | tf_op jit(solution)/shard_map/ppermute | solution.py:407
  91.0 1.0 slice.234
  92.0 1.1 slice.235
  93.1 1.9 %pad_maximum_fusion.1 = (f32[5,256,256]{2,1,0:T(8,128)}, f32[5,256,256]{2,1,0:T(8,128)S(1)}, f32[5,256,256]{2,1,0:T(8,128)}) fusion(f32[2,256,256]{2,1,0:T(8,128)S(1)} %slice.235, f32[2,256,256]{2,1,0:T(8,128)S(1)} %copy-done.21, f32[1,256,256]{2,1,0:T(8,128)S(1)} %slice.234, f32[2,256,256]{2,1,0:T(8,128)S(1)} %get-tuple-element.73, ...), kind=kLoop, calls=%fused_computation.2 | loop fusion | flops 1638400 | bytes 6553601 | tf_op jit(solution)/shard_map/concatenate | solution.py:512
  95.0 1.9 %collective-permute-start.15 = (f32[5,256,256]{2,1,0:T(8,128)S(1)}, f32[5,256,256]{2,1,0:T(8,128)}, u32[]{:S(2)}, u32[]{:S(2)}) collective-permute-start(f32[5,256,256]{2,1,0:T(8,128)S(1)} %get-tuple-element.66.refs_5_), channel_id=1, source_target_pairs={{4,5},{13,12},{22,23},{31,30},{18,19},{27,26}} | collective-permute-start | bytes 3932168 | tf_op jit(solution)/shard_map/ppermute | solution.py:407
  97.0 3.1 %fusion.2 = (f32[5,256,256]{2,1,0:T(8,128)S(1)}, f32[5,256,256]{2,1,0:T(8,128)}) fusion(f32[5,256,256]{2,1,0:T(8,128)} %collective-permute-done.11, f32[2,256,256]{2,1,0:T(8,128)S(1)} %copy-done.15, f32[2,256,256]{2,1,0:T(8,128)S(1)} %collective-permute-done.3, f32[1,256,256]{2,1,0:T(8,128)S(1)} %slice.238, f32[2,256,256]{2,1,0:T(8,128)S(1)} %slice-done.6, ...), kind=kLoop, calls=%fused_computation.6 | loop fusion | flops 4259840 | bytes 10485765 | tf_op jit(solution)/shard_map/jit(_where)/select_n | solution.py:522
  100.1 0.6 collective-permute-start.18
  100.7 0.1 stack.134.refs_0_
  100.8 1.5 %collective-permute-start.10 = (f32[2,256,256]{2,1,0:T(8,128)}, f32[2,256,256]{2,1,0:T(8,128)}, u32[]{:S(2)}, u32[]{:S(2)}) collective-permute-start(f32[2,256,256]{2,1,0:T(8,128)} %collective-permute-done.9), channel_id=1, source_target_pairs={{4,6},{5,7},{12,14},{13,15},{20,22},{21,23},{28,30},{29,31}} | collective-permute-start | bytes 1572872 | tf_op jit(solution)/shard_map/ppermute | solution.py:407
  102.3 1.4 %collective-permute-done.18 = f32[5,128,128]{2,1,0:T(8,128)} collective-permute-done((f32[5,128,128]{2,1,0:T(8,128)S(1)}, f32[5,128,128]{2,1,0:T(8,128)}, u32[]{:S(2)}, u32[]{:S(2)}) %collective-permute-start.18) | collective-permute-done | bytes 327712 | tf_op jit(solution)/shard_map/ppermute | solution.py:407
  103.7 1.1 broadcast_select_fusion.9
  104.8 0.0 copy-start
  104.8 0.1 slice_bitcast_fusion.10
  105.0 1.1 copy-done
  106.1 0.4 copy-done.1
  106.5 13.2 %shard_map.32 = (f32[2560,1280]{1,0:T(8,128)}, bf16[512,1280]{1,0:T(8,128)(2,1)S(1)}, bf16[512,1280]{1,0:T(8,128)(2,1)S(1)}) custom-call(s32[7]{0:T(128)S(1)} %stack.134.refs_0_, f32[2560,1280]{1,0:T(8,128)} %refs_1_.5, f32[10,1,256]{2,1,0:T(1,128)S(1)} %reshape.17.refs_2_, f32[5,256,256]{2,1,0:T(8,128)S(1)} %get-tuple-element.61.refs_3_, ...), custom_call_target="tpu_custom_call" | custom-call | flops 5536481280 | bytes 13107200 | tf_op jit(solution)/shard_map/pallas_call | solution.py:277
  119.7 3.7 %select_select_fusion = (f32[2,256,256]{2,1,0:T(8,128)S(1)}, f32[2,256,256]{2,1,0:T(8,128)}) fusion(f32[2,256,256]{2,1,0:T(8,128)} %copy-done.12, f32[2,256,256]{2,1,0:T(8,128)} %copy-done.14, f32[2,256,256]{2,1,0:T(8,128)} %collective-permute-done.9, pred[]{:T(512)S(6)} %eq.76, pred[]{:T(512)S(6)} %eq.32, f32[2,256,256]{2,1,0:T(8,128)} %collective-permute-done.10, ...), kind=kLoop, calls=%fused_computation.18 | loop fusion | flops 786432 | bytes 4194308 | tf_op jit(solution)/shard_map/jit(_where)/select_n | solution.py:541
  123.5 0.2 fusion.3.refs_3_
  123.6 0.2 collective-permute-start.20
  123.8 0.4 collective-permute-start.19
  124.2 0.1 stack.122.refs_0_
  124.4 0.1 slice.255.refs_5_
  124.4 1.2 slice.252.refs_6_
  125.7 1.2 slice.256.refs_6_
  126.9 6.2 %shard_map.33.refs_14_ = f32[2560,1280]{1,0:T(8,128)} custom-call(s32[7]{0:T(128)S(1)} %stack.122.refs_0_, f32[2560,1280]{1,0:T(8,128)} %refs_1_.5, f32[10,1,256]{2,1,0:T(1,128)S(1)} %reshape.17.refs_2_, f32[3,256,256]{2,1,0:T(8,128)S(1)} %fusion.3.refs_3_, f32[3,256,256]{2,1,0:T(8,128)} %collective-permute-done.20.refs_4_, ...), custom_call_target="tpu_custom_call", output_to_operand_aliasing={{}: (14, {})} | custom-call | flops 2415919104 | bytes 7864320 | tf_op jit(solution)/shard_map/pallas_call | solution.py:277
  133.2 5.9 %shard_map.34 = f32[2560,1280]{1,0:T(8,128)} custom-call(s32[7]{0:T(128)S(1)} %stack.122.refs_0_, f32[2560,1280]{1,0:T(8,128)} %refs_1_.5, f32[10,1,256]{2,1,0:T(1,128)S(1)} %reshape.17.refs_2_, f32[2,256,256]{2,1,0:T(8,128)} %get-tuple-element.71.refs_3_, f32[2,256,256]{2,1,0:T(8,128)} %collective-permute-done.19.refs_4_, ...), custom_call_target="tpu_custom_call", output_to_operand_aliasing={{}: (14, {})} | custom-call | flops 1610612736 | bytes 5242880 | tf_op jit(solution)/shard_map/pallas_call | solution.py:277
  (104 shorter events, 0.7 us)
Async XLA Ops:
  1.8 14.9 %copy-start.22 = (f32[1,128,128]{2,1,0:T(8,128)}, f32[1,128,128]{2,1,0:T(8,128)S(1)}, u32[]{:S(2)}) copy-start(f32[1,128,128]{2,1,0:T(8,128)S(1)} %get-tuple-element.100) | copy-start | bytes 196612
  2.5 14.2 %collective-permute-start = (f32[3,128,128]{2,1,0:T(8,128)}, f32[3,128,128]{2,1,0:T(8,128)S(1)}, u32[]{:S(2)}, u32[]{:S(2)}) collective-permute-start(f32[3,128,128]{2,1,0:T(8,128)} %pad_maximum_fusion.4), channel_id=1, source_target_pairs={{0,16},{1,17},{8,24},{9,25}} | collective-permute-start | bytes 589832 | tf_op jit(solution)/shard_map/ppermute | solution.py:407
  7.4 1.3 slice-start.4
  11.1 20.0 %collective-permute-start.3 = (f32[2,256,256]{2,1,0:T(8,128)}, f32[2,256,256]{2,1,0:T(8,128)S(1)}, u32[]{:S(2)}, u32[]{:S(2)}) collective-permute-start(f32[2,256,256]{2,1,0:T(8,128)} %fusion.5), channel_id=1, source_target_pairs={{0,2},{1,3},{8,10},{9,11},{4,6},{12,7},{5,14},{13,15}} | collective-permute-start | bytes 1572872 | tf_op jit(solution)/shard_map/ppermute | solution.py:407
  15.0 40.9 %collective-permute-start.11 = (f32[5,256,256]{2,1,0:T(8,128)}, f32[5,256,256]{2,1,0:T(8,128)}, u32[]{:S(2)}, u32[]{:S(2)}) collective-permute-start(f32[5,256,256]{2,1,0:T(8,128)} %slice_bitcast_fusion), channel_id=1, source_target_pairs={{16,18},{17,19},{24,26},{25,27}} | collective-permute-start | bytes 3932168 | tf_op jit(solution)/shard_map/ppermute | solution.py:407
  16.7 3.4 %copy-start.23 = (f32[3,128,128]{2,1,0:T(8,128)}, f32[3,128,128]{2,1,0:T(8,128)S(1)}, u32[]{:S(2)}) copy-start(f32[3,128,128]{2,1,0:T(8,128)S(1)} %collective-permute-done) | copy-start | bytes 589828
  16.7 8.4 %collective-permute-start.1 = (f32[3,128,128]{2,1,0:T(8,128)S(1)}, f32[3,128,128]{2,1,0:T(8,128)}, u32[]{:S(2)}, u32[]{:S(2)}) collective-permute-start(f32[3,128,128]{2,1,0:T(8,128)S(1)} %broadcast_select_fusion.12), channel_id=1, source_target_pairs={{0,8},{1,9},{8,0},{9,1},{16,24},{17,25},{24,16},{25,17}} | collective-permute-start | bytes 589832 | tf_op jit(solution)/shard_map/ppermute | solution.py:407
  20.1 15.2 %collective-permute-start.5 = (f32[2,256,256]{2,1,0:T(8,128)S(1)}, f32[2,256,256]{2,1,0:T(8,128)}, u32[]{:S(2)}, u32[]{:S(2)}) collective-permute-start(f32[2,256,256]{2,1,0:T(8,128)S(1)} %bitcast.114), channel_id=1, source_target_pairs={{0,16},{1,17},{2,18},{3,19},{4,20},{5,21},{6,22},{7,23},{8,24},{9,... | collective-permute-start | bytes 1572872 | tf_op jit(solution)/shard_map/ppermute | solution.py:407
  26.1 11.8 %collective-permute-start.2 = (f32[2,3,128,128]{3,2,1,0:T(8,128)S(1)}, f32[2,3,128,128]{3,2,1,0:T(8,128)S(1)}, u32[]{:S(2)}, u32[]{:S(2)}) collective-permute-start(f32[2,3,128,128]{3,2,1,0:T(8,128)S(1)} %pad_maximum_fusion.3), channel_id=1, source_target_pairs={{0,1},{1,0},{8,9},{9,8},{16,17},{17,16},{24,25},{25,24}} | collective-permute-start | bytes 1179656 | tf_op jit(solution)/shard_map/ppermute | solution.py:407
  28.1 24.8 %collective-permute-start.4 = (f32[3,256,256]{2,1,0:T(8,128)S(1)}, f32[3,256,256]{2,1,0:T(8,128)S(1)}, u32[]{:S(2)}, u32[]{:S(2)}) collective-permute-start(f32[3,256,256]{2,1,0:T(8,128)S(1)} %pad_maximum_fusion.2), channel_id=1, source_target_pairs={{0,16},{1,17},{2,18},{3,19},{4,20},{5,21},{6,22},{7,23},{8,24},{9,... | collective-permute-start | bytes 2359304 | tf_op jit(solution)/shard_map/ppermute | solution.py:407
  31.1 65.8 %copy-start.12 = (f32[2,256,256]{2,1,0:T(8,128)}, f32[2,256,256]{2,1,0:T(8,128)S(1)}, u32[]{:S(2)}) copy-start(f32[2,256,256]{2,1,0:T(8,128)S(1)} %collective-permute-done.3) | copy-start | bytes 1572868
  36.6 56.5 %copy-start.16 = (f32[2,256,256]{2,1,0:T(8,128)}, f32[2,256,256]{2,1,0:T(8,128)S(1)}, u32[]{:S(2)}) copy-start(f32[2,256,256]{2,1,0:T(8,128)S(1)} %get-tuple-element.44) | copy-start | bytes 1572868
  36.6 17.1 %collective-permute-start.8 = (f32[2,256,256]{2,1,0:T(8,128)S(1)}, f32[2,256,256]{2,1,0:T(8,128)S(1)}, u32[]{:S(2)}, u32[]{:S(2)}) collective-permute-start(f32[2,256,256]{2,1,0:T(8,128)S(1)} %get-tuple-element.63), channel_id=1, source_target_pairs={{0,2},{1,3},{8,10},{9,11},{2,4},{3,5},{10,12},{11,13},{18,20},{26,... | collective-permute-start | bytes 1572872 | tf_op jit(solution)/shard_map/ppermute | solution.py:407
  42.1 13.7 %collective-permute-start.13 = (f32[2,256,256]{2,1,0:T(8,128)S(1)}, f32[2,256,256]{2,1,0:T(8,128)S(1)}, u32[]{:S(2)}, u32[]{:S(2)}) collective-permute-start(f32[2,256,256]{2,1,0:T(8,128)S(1)} %get-tuple-element.44), channel_id=1, source_target_pairs={{4,2},{12,3},{5,10},{13,11},{22,20},{30,21},{23,28},{31,29}} | collective-permute-start | bytes 1572872 | tf_op jit(solution)/shard_map/ppermute | solution.py:407
  43.0 10.8 %collective-permute-start.6 = (f32[2,256,256]{2,1,0:T(8,128)S(1)}, f32[2,256,256]{2,1,0:T(8,128)S(1)}, u32[]{:S(2)}, u32[]{:S(2)}) collective-permute-start(f32[2,256,256]{2,1,0:T(8,128)S(1)} %get-tuple-element.44), channel_id=1, source_target_pairs={{0,8},{1,9},{2,10},{3,11},{4,12},{5,13},{6,14},{7,15},{8,0},{9,1},... | collective-permute-start | bytes 1572872 | tf_op jit(solution)/shard_map/ppermute | solution.py:407
  47.0 0.7 copy-start.6
  53.0 19.9 %collective-permute-start.12 = (f32[3,256,256]{2,1,0:T(8,128)S(1)}, f32[3,256,256]{2,1,0:T(8,128)S(1)}, u32[]{:S(2)}, u32[]{:S(2)}) collective-permute-start(f32[3,256,256]{2,1,0:T(8,128)S(1)} %broadcast_select_fusion.2), channel_id=1, source_target_pairs={{4,2},{12,3},{5,10},{13,11},{22,20},{30,21},{23,28},{31,29}} | collective-permute-start | bytes 2359304 | tf_op jit(solution)/shard_map/ppermute | solution.py:407
  53.8 38.2 %copy-start.14 = (f32[2,256,256]{2,1,0:T(8,128)}, f32[2,256,256]{2,1,0:T(8,128)S(1)}, u32[]{:S(2)}) copy-start(f32[2,256,256]{2,1,0:T(8,128)S(1)} %collective-permute-done.8) | copy-start | bytes 1572868
  53.8 6.6 %copy-start.20 = (f32[2,256,256]{2,1,0:T(8,128)}, f32[2,256,256]{2,1,0:T(8,128)S(1)}, u32[]{:S(2)}) copy-start(f32[2,256,256]{2,1,0:T(8,128)S(1)} %collective-permute-done.6) | copy-start | bytes 1572868
  53.8 19.2 %collective-permute-start.7 = (f32[3,256,256]{2,1,0:T(8,128)S(1)}, f32[3,256,256]{2,1,0:T(8,128)}, u32[]{:S(2)}, u32[]{:S(2)}) collective-permute-start(f32[3,256,256]{2,1,0:T(8,128)S(1)} %broadcast_select_fusion.2), channel_id=1, source_target_pairs={{0,8},{1,9},{2,10},{3,11},{4,12},{5,13},{6,14},{7,15},{8,0},{9,1},... | collective-permute-start | bytes 2359304 | tf_op jit(solution)/shard_map/ppermute | solution.py:407
  55.9 4.6 %copy-start.24 = (f32[2,256,256]{2,1,0:T(8,128)}, f32[2,256,256]{2,1,0:T(8,128)S(1)}, u32[]{:S(2)}) copy-start(f32[2,256,256]{2,1,0:T(8,128)S(1)} %collective-permute-done.13) | copy-start | bytes 1572868
  59.7 0.7 copy-start.9
  60.5 12.4 %collective-permute-start.16 = (f32[5,128,128]{2,1,0:T(8,128)S(1)}, f32[5,128,128]{2,1,0:T(8,128)}, u32[]{:S(2)}, u32[]{:S(2)}) collective-permute-start(f32[5,128,128]{2,1,0:T(8,128)S(1)} %broadcast_select_fusion.11), channel_id=1, source_target_pairs={{0,4},{1,5},{8,12},{9,13},{16,20},{17,21},{24,28},{25,29}} | collective-permute-start | bytes 983048 | tf_op jit(solution)/shard_map/ppermute | solution.py:407
  67.0 29.9 %copy-start.17 = (f32[1,256,256]{2,1,0:T(8,128)}, f32[1,256,256]{2,1,0:T(8,128)S(1)}, u32[]{:S(2)}) copy-start(f32[1,256,256]{2,1,0:T(8,128)S(1)} %slice.238) | copy-start | bytes 786436
  68.0 32.8 %collective-permute-start.9 = (f32[2,256,256]{2,1,0:T(8,128)}, f32[2,256,256]{2,1,0:T(8,128)}, u32[]{:S(2)}, u32[]{:S(2)}) collective-permute-start(f32[2,256,256]{2,1,0:T(8,128)} %get-tuple-element.72), channel_id=1, source_target_pairs={{2,4},{3,5},{10,12},{11,13},{18,20},{26,21},{19,28},{27,29},{4,6},... | collective-permute-start | bytes 1572872 | tf_op jit(solution)/shard_map/ppermute | solution.py:407
  73.0 20.1 %copy-start.19 = (f32[3,256,256]{2,1,0:T(8,128)}, f32[3,256,256]{2,1,0:T(8,128)S(1)}, u32[]{:S(2)}) copy-start(f32[3,256,256]{2,1,0:T(8,128)S(1)} %collective-permute-done.12) | copy-start | bytes 2359300
  73.0 20.1 %copy-start.21 = (f32[2,256,256]{2,1,0:T(8,128)S(1)}, f32[2,256,256]{2,1,0:T(8,128)}, u32[]{:S(2)}) copy-start(f32[2,256,256]{2,1,0:T(8,128)} %copy-done.20) | copy-start | bytes 1572868
  73.0 27.0 %collective-permute-start.17 = (f32[5,128,128]{2,1,0:T(8,128)S(1)}, f32[5,128,128]{2,1,0:T(8,128)S(1)}, u32[]{:S(2)}, u32[]{:S(2)}) collective-permute-start(f32[5,128,128]{2,1,0:T(8,128)S(1)} %broadcast_select_fusion.7), channel_id=1, source_target_pairs={{0,2},{1,3},{4,6},{5,7},{8,10},{9,11},{12,14},{13,15},{16,18},{17,... | collective-permute-start | bytes 983048 | tf_op jit(solution)/shard_map/ppermute | solution.py:407
  93.1 3.9 %copy-start.15 = (f32[2,256,256]{2,1,0:T(8,128)S(1)}, f32[2,256,256]{2,1,0:T(8,128)}, u32[]{:S(2)}) copy-start(f32[2,256,256]{2,1,0:T(8,128)} %copy-done.14) | copy-start | bytes 1572868
  93.1 3.8 %slice-start.5 = ((f32[3,256,256]{2,1,0:T(8,128)}), f32[1,256,256]{2,1,0:T(8,128)S(1)}, s32[]{:S(2)}) async-start(f32[3,256,256]{2,1,0:T(8,128)} %copy-done.19), calls=%async_computation.5 | async-start | bytes 524288 | tf_op jit(solution)/shard_map/slice | solution.py:512
  93.1 3.8 %slice-start.6 = ((f32[3,256,256]{2,1,0:T(8,128)}), f32[2,256,256]{2,1,0:T(8,128)S(1)}, s32[]{:S(2)}) async-start(f32[3,256,256]{2,1,0:T(8,128)} %copy-done.19), calls=%async_computation.6 | async-start | bytes 1048576 | tf_op jit(solution)/shard_map/slice | solution.py:512
  93.1 3.8 %copy-start.25 = (f32[2,256,256]{2,1,0:T(8,128)S(1)}, f32[2,256,256]{2,1,0:T(8,128)}, u32[]{:S(2)}) copy-start(f32[2,256,256]{2,1,0:T(8,128)} %copy-done.24) | copy-start | bytes 1572868
  95.0 5.6 %copy-start.26 = (f32[2560]{0:T(1024)S(1)}, f32[2560]{0:T(1024)}, u32[]{:S(2)}) copy-start(f32[2560]{0:T(1024)} %param.3) | copy-start | bytes 30724
  95.0 9.9 %collective-permute-start.15 = (f32[5,256,256]{2,1,0:T(8,128)S(1)}, f32[5,256,256]{2,1,0:T(8,128)}, u32[]{:S(2)}, u32[]{:S(2)}) collective-permute-start(f32[5,256,256]{2,1,0:T(8,128)S(1)} %get-tuple-element.66.refs_5_), channel_id=1, source_target_pairs={{4,5},{13,12},{22,23},{31,30},{18,19},{27,26}} | collective-permute-start | bytes 3932168 | tf_op jit(solution)/shard_map/ppermute | solution.py:407
  100.0 4.9 %collective-permute-start.14 = (f32[5,256,256]{2,1,0:T(8,128)S(1)}, f32[5,256,256]{2,1,0:T(8,128)}, u32[]{:S(2)}, u32[]{:S(2)}) collective-permute-start(f32[5,256,256]{2,1,0:T(8,128)S(1)} %get-tuple-element.61.refs_3_), channel_id=1, source_target_pairs={{0,1},{1,0},{2,3},{3,2},{4,5},{5,4},{6,7},{7,6},{8,9},{9,8},{10,11... | collective-permute-start | bytes 3932168 | tf_op jit(solution)/shard_map/ppermute | solution.py:407
  100.1 3.6 %collective-permute-start.18 = (f32[5,128,128]{2,1,0:T(8,128)S(1)}, f32[5,128,128]{2,1,0:T(8,128)}, u32[]{:S(2)}, u32[]{:S(2)}) collective-permute-start(f32[5,128,128]{2,1,0:T(8,128)S(1)} %broadcast_select_fusion.8), channel_id=1, source_target_pairs={{0,1},{1,0},{2,3},{3,2},{4,5},{5,4},{6,7},{7,6},{8,9},{9,8},{10,11... | collective-permute-start | bytes 983048 | tf_op jit(solution)/shard_map/ppermute | solution.py:407
  100.8 18.9 %collective-permute-start.10 = (f32[2,256,256]{2,1,0:T(8,128)}, f32[2,256,256]{2,1,0:T(8,128)}, u32[]{:S(2)}, u32[]{:S(2)}) collective-permute-start(f32[2,256,256]{2,1,0:T(8,128)} %collective-permute-done.9), channel_id=1, source_target_pairs={{4,6},{5,7},{12,14},{13,15},{20,22},{21,23},{28,30},{29,31}} | collective-permute-start | bytes 1572872 | tf_op jit(solution)/shard_map/ppermute | solution.py:407
  103.7 1.3 copy-start.7
  103.7 1.3 copy-start.10
  104.8 1.3 copy-start
  104.8 1.7 %copy-start.1 = (f32[5,256,256]{2,1,0:T(8,128)S(1)}, f32[5,256,256]{2,1,0:T(8,128)}, u32[]{:S(2)}) copy-start(f32[5,256,256]{2,1,0:T(8,128)} %get-tuple-element.67) | copy-start | bytes 3932164
  104.9 18.5 %slice-start = ((s8[13107200]{0:T(1024)(128)(4,1)}), s8[4194304]{0:T(1024)(128)(4,1)S(1)}, s32[]{:S(2)}) async-start(s8[13107200]{0:T(1024)(128)(4,1)} %bitcast.108), calls=%async_computation | async-start | bytes 8388608
  106.5 16.9 %slice-start.1 = ((s8[13107200]{0:T(1024)(128)(4,1)}), s8[4194304]{0:T(1024)(128)(4,1)S(1)}, s32[]{:S(2)}) async-start(s8[13107200]{0:T(1024)(128)(4,1)} %bitcast.108), calls=%async_computation.1 | async-start | bytes 8388608
  106.5 16.9 %slice-start.2 = ((s8[13107200]{0:T(1024)(128)(4,1)}), s8[4194304]{0:T(1024)(128)(4,1)S(1)}, s32[]{:S(2)}) async-start(s8[13107200]{0:T(1024)(128)(4,1)} %bitcast.108), calls=%async_computation.2 | async-start | bytes 8388608
  106.5 17.0 %slice-start.3 = ((s8[13107200]{0:T(1024)(128)(4,1)}), s8[524288]{0:T(1024)(128)(4,1)S(1)}, s32[]{:S(2)}) async-start(s8[13107200]{0:T(1024)(128)(4,1)} %bitcast.108), calls=%async_computation.3 | async-start | bytes 1048576
  119.7 3.8 %copy-start.2 = (bf16[512,1280]{1,0:T(8,128)(2,1)}, bf16[512,1280]{1,0:T(8,128)(2,1)S(1)}, u32[]{:S(2)}) copy-start(bf16[512,1280]{1,0:T(8,128)(2,1)S(1)} %get-tuple-element.57.refs_12_) | copy-start | bytes 3932164
  119.7 3.7 %copy-start.4 = (bf16[512,1280]{1,0:T(8,128)(2,1)}, bf16[512,1280]{1,0:T(8,128)(2,1)S(1)}, u32[]{:S(2)}) copy-start(bf16[512,1280]{1,0:T(8,128)(2,1)S(1)} %get-tuple-element.59.refs_13_) | copy-start | bytes 3932164
  119.7 3.8 %copy-start.13 = (f32[5,256,256]{2,1,0:T(8,128)S(1)}, f32[5,256,256]{2,1,0:T(8,128)}, u32[]{:S(2)}) copy-start(f32[5,256,256]{2,1,0:T(8,128)} %get-tuple-element.62) | copy-start | bytes 3932164
  119.7 3.8 %copy-start.18 = (f32[1,256,256]{2,1,0:T(8,128)S(1)}, f32[1,256,256]{2,1,0:T(8,128)}, u32[]{:S(2)}) copy-start(f32[1,256,256]{2,1,0:T(8,128)} %copy-done.17) | copy-start | bytes 786436
  123.6 3.2 %collective-permute-start.20 = (f32[3,256,256]{2,1,0:T(8,128)S(1)}, f32[3,256,256]{2,1,0:T(8,128)}, u32[]{:S(2)}, u32[]{:S(2)}) collective-permute-start(f32[3,256,256]{2,1,0:T(8,128)S(1)} %fusion.3.refs_3_), channel_id=1, source_target_pairs={{0,1},{1,0},{2,3},{3,2},{4,5},{5,4},{6,7},{7,6},{8,9},{9,8},{10,11... | collective-permute-start | bytes 2359304 | tf_op jit(solution)/shard_map/ppermute | solution.py:407
  123.8 9.3 %collective-permute-start.19 = (f32[2,256,256]{2,1,0:T(8,128)}, f32[2,256,256]{2,1,0:T(8,128)}, u32[]{:S(2)}, u32[]{:S(2)}) collective-permute-start(f32[2,256,256]{2,1,0:T(8,128)} %get-tuple-element.71.refs_3_), channel_id=1, source_target_pairs={{0,1},{1,0},{2,3},{3,2},{4,5},{5,4},{6,7},{7,6},{8,9},{9,8},{10,11... | collective-permute-start | bytes 1572872 | tf_op jit(solution)/shard_map/ppermute | solution.py:407
  124.3 2.5 %copy-start.8 = (f32[256,256]{1,0:T(8,128)S(1)}, f32[256,256]{1,0:T(8,128)}, u32[]{:S(2)}) copy-start(f32[256,256]{1,0:T(8,128)} %copy-done.6) | copy-start | bytes 786436
  124.4 2.5 %copy-start.11 = (f32[256,256]{1,0:T(8,128)S(1)}, f32[256,256]{1,0:T(8,128)}, u32[]{:S(2)}) copy-start(f32[256,256]{1,0:T(8,128)} %copy-done.9) | copy-start | bytes 786436
  124.4 2.5 %copy-start.3 = (bf16[512,1280]{1,0:T(8,128)(2,1)S(1)}, bf16[512,1280]{1,0:T(8,128)(2,1)}, u32[]{:S(2)}) copy-start(bf16[512,1280]{1,0:T(8,128)(2,1)} %copy-done.2) | copy-start | bytes 3932164
  124.4 2.5 %copy-start.5 = (bf16[512,1280]{1,0:T(8,128)(2,1)S(1)}, bf16[512,1280]{1,0:T(8,128)(2,1)}, u32[]{:S(2)}) copy-start(bf16[512,1280]{1,0:T(8,128)(2,1)} %copy-done.4) | copy-start | bytes 3932164

commit v2 on v1

--- a/solution.py
+++ b/solution.py
@@ -176,13 +176,17 @@
     return left, right
 
 
-def update_kernel(n_row, n_col, step_of, count, given, *refs):
+def in_order(middle, others):
+    return jnp.concatenate([others[:1], middle[...], others[1:]], axis=0).reshape(-1, NB)
+
+
+def update_kernel(n_row, n_col, step_of, count, first_block, col_parts, *refs):
     (place, matrix, noise, own, twin, here, there) = refs[:7]
     (first_factor, first_inverse, cross, second_factor, second_inverse) = refs[7:12]
     refs = refs[12:]
-    if given is None:
-        mine, other, out, high, low = refs[:5]
-        refs = refs[5:]
+    if col_parts:
+        raw_cols, (out, high, low) = refs[:col_parts], refs[col_parts : col_parts + 3]
+        refs = refs[col_parts + 3 :]
     else:
         high, low, _, out = refs[:4]
         refs = refs[4:]
@@ -207,14 +211,19 @@
         wide_right(cross[...]),
         wide_right(second_inverse[...]),
     )
-    if given is None:
+    if col_parts:
         odd = place[1] == 1
+        if col_parts == 2:
+            mine, other = raw_cols[0][...], raw_cols[1][...]
+        else:
+            mine, other = in_order(*raw_cols[:2]), in_order(*raw_cols[2:])
         left, right = solve_both(
-            jnp.where(odd, other[...], mine[...]), jnp.where(odd, mine[...], other[...]), *inverses
+            jnp.where(odd, other, mine), jnp.where(odd, mine, other), *inverses
         )
         high[:NB], low[:NB] = split(left.T)
         high[NB:], low[NB:] = split(right.T)
-    by_columns = jnp.where(place[5] == 1, here[...], there[...])
+    part = slice(first_block, first_block + count)
+    by_columns = jnp.where(place[5] == 1, here[part], there[part])
     by_core = jnp.where(place[6] == 0, twin[...], own[...])
     first = jnp.where(place[3] == 1, own[...], twin[...])
     second = jnp.where(place[4] == 1, by_columns, by_core)
@@ -265,7 +274,9 @@
         leave(r).wait()
 
 
-def update(place, step_of, count, matrix, noise, rows, factored, n_row, n_col, cols=None, done=None):
+def update(
+    place, step_of, count, matrix, noise, rows, factored, n_row, n_col, first_block=0, cols=(), done=None
+):
     cols_local = matrix.shape[1]
     whole = pl.BlockSpec(memory_space=pltpu.VMEM)
     anywhere = pl.BlockSpec(memory_space=pl.ANY)
@@ -275,10 +286,10 @@
     solved = count + (cols_local // NB if done is None else 0)
     flops = 2 * 3 * NB * NB * (solved * 3 * NB + count * cols_local)
     outs = pl.pallas_call(
-        functools.partial(update_kernel, n_row, n_col, step_of, count, done),
+        functools.partial(update_kernel, n_row, n_col, step_of, count, first_block, len(cols)),
         in_specs=[pl.BlockSpec(memory_space=pltpu.SMEM), anywhere]
         + [whole] * 10
-        + ([whole, whole] if done is None else [whole, whole, anywhere]),
+        + ([whole] * len(cols) if done is None else [whole, whole, anywhere]),
         out_specs=[anywhere, whole, whole] if done is None else anywhere,
         out_shape=[result, part, part] if done is None else result,
         scratch_shapes=[
@@ -295,6 +306,46 @@
         ),
     )(place, matrix, noise, *rows, *factored, *extra)
     return outs if done is None else (outs, *done[1:])
+
+
+def pick_kernel(cases, which, *refs):
+    sources, out, sems = refs[:-2], refs[-2], refs[-1]
+    for number, case in enumerate(cases):
+
+        @pl.when(which[0] == number)
+        def _():
+            copies = [
+                pltpu.make_async_copy(sources[k].at[at], out.at[b], sems.at[b])
+                for b, (k, at) in enumerate(case)
+            ]
+            for copy in copies:
+                copy.start()
+            for copy in copies:
+                copy.wait()
+
+
+def pick(cases):
+    sources, lists, which = [], [], jnp.int32(len(cases) - 1)
+    for condition, case in cases:
+        places = []
+        for array, at in case:
+            known = [k for k, x in enumerate(sources) if x is array]
+            if not known:
+                sources.append(array)
+            places.append((known[0] if known else len(sources) - 1, at))
+        lists.append(places)
+    for number in reversed(range(len(cases) - 1)):
+        which = jnp.where(cases[number][0], number, which)
+    count = len(lists[0])
+    return pl.pallas_call(
+        functools.partial(pick_kernel, lists),
+        in_specs=[pl.BlockSpec(memory_space=pltpu.SMEM)]
+        + [pl.BlockSpec(memory_space=pl.ANY)] * len(sources),
+        out_specs=pl.BlockSpec(memory_space=pltpu.VMEM),
+        out_shape=jax.ShapeDtypeStruct((count, NB, NB), jnp.float32),
+        scratch_shapes=[pltpu.SemaphoreType.DMA((count,))],
+        cost_estimate=pl.CostEstimate(flops=0, bytes_accessed=0, transcendentals=0),
+    )(which.astype(jnp.int32).reshape(1), *sources)
 
 
 def start_factor(corner):
@@ -482,8 +533,8 @@
 
     others = after(others, lead_x)
     y2 = route(others, along_y)
-    mine1 = jnp.where(low_line, after(middle, lead_x), y1)
-    x1 = route(after(mine1, begun[0]), along_x)
+    mine1 = after(jnp.where(low_line, after(middle, lead_x), y1), begun[0])
+    x1 = route(mine1, along_x)
 
     h2 = route(
         jnp.where(
@@ -493,103 +544,117 @@
         ),
         up(0, low) + up(1, low) + side + lift,
     )
-    down = [((s, 4 + r), (r, 2 + s)) for r in low for s in (0, 1)]
-    down += [((2 + s, 4 + r), (r, 4 + s)) for r in high for s in (0, 1)]
-    d1 = route(after(mine1, begun[0]), down)
-    e1 = route(odd(slice(0, n_cols)), up(0, high))
-    factored = finish_factor(begun, *rest, before_last=(x1, h2, y2, d1, e1))
-    mine2 = jnp.where(low_line, after(others, factored[2]), y2)
+    homes = {0: (0, 4), 1: (1, 5), 2: (2, 6), 3: (3, 7)}
+    down = [(at, (r, at[1] - 2)) for r, at in homes.items()]
+    down_other = [(at, (r, (at[1] - 2) ^ 1)) for r, at in homes.items()]
+    mine_down1 = route(mine1, down)
+    risen = route(after(odd(slice(0, n_cols)), lead_x), up(0, high))
+    factored = finish_factor(begun, *rest, before_last=(x1, h2, y2))
+    cross = factored[2]
+    mine2 = jnp.where(low_line, after(others, cross), y2)
     x2 = route(after(mine2, x1), along_x)
-    d2 = route(mine2, down)
-    h2 = after(h2, factored[2])
+    mine_down2 = route(mine2, down)
+    other_down1 = route(after(x1, cross), down_other)
+    other_down2 = route(x2, down_other)
+    h2 = after(h2, cross)
     h3 = route(
         jnp.where((plane == 1) & ~low_line, mine2[1:], h2), up(1, low) + side + up(2, low + high)
     )
     h4 = route(h3, up(2, low + high))
-    inverses = spread_inverses(factored, (h2,), (x2,), plane, core)
-    factored = (factored[0], inverses[0], inverses[1], factored[3], inverses[2])
-
-    given = lambda x, y: jnp.concatenate([y[:1], x, y[1:]], axis=0)
-    col_mine = given(mine1, mine2)
-    col_given = given(x1, x2)
-    first_cols = jnp.where(is_even, col_mine, col_given)
-    second_cols = jnp.where(is_even, col_given, col_mine)
-    homes = [((r, c), (r, c ^ 1)) for r, c in [(0, 4), (1, 5), (2, 6), (3, 7), (2, 2), (3, 3)]]
-    second_twin = route(second_cols, homes)
+    inverses = spread_inverses(
+        factored, (h2, risen, mine_down1), (x2, h3, mine_down2, other_down1), plane, core
+    )
+    factored = (factored[0], inverses[0], inverses[1], factored[3], after(inverses[2], h4))
 
     by_odd = (low_line & (plane == 2)) | (~low_line & (plane == 3))
     by_even = ~low_line & (plane == 1)
-    own_1 = jnp.where(
-        by_odd,
-        first_cols,
-        jnp.where(
-            plane == 0,
-            odd(slice(0, n_cols)),
-            jnp.where(
-                by_even,
-                e1,
-                jnp.where(plane == 3, jnp.concatenate([h1[:1], h1, h2], axis=0), given(d1, d2)),
-            ),
-        ),
-    )
-    own_2 = jnp.where(
-        plane == 0,
-        even(slice(0, 1 + cut)),
-        jnp.where(
-            by_even,
-            first_cols[: 1 + cut],
-            given(jnp.where(plane == 1, h1, jnp.where(plane == 2, h2, h3)), h1[:1]),
-        ),
-    )
-
-    def rows(own, part):
-        return own, route(own, TWINS), second_cols[part], second_twin[part]
+
+    def local(steps):
+        return [(kernel, (pl.ds(NB * t, NB), pl.ds(0, NB))) for t in steps]
+
+    def ordered(mid, rest, part):
+        whole = [(rest, 0)] + [(mid, c) for c in range(cut)] + [(rest, 1 + c) for c in range(cut)]
+        return whole[part]
+
+    def simple(x, steps):
+        return [(x, c) for c in steps]
+
+    everything, start = slice(0, n_cols), slice(0, 1 + cut)
+    second_cols = pick(
+        [(is_even, ordered(x1, x2, everything)), (None, ordered(mine1, mine2, everything))]
+    )
+    col_homes = [(at, (at[0], at[1] ^ 1)) for at in (*homes.values(), (2, 2), (3, 3))]
+    second_twin = route(second_cols, col_homes)
+    clipped = [max(c - 1, 0) for c in range(1 + cut)]
+    own_early = pick(
+        [
+            (plane == 0, local(range(0, 2 + 2 * cut, 2))),
+            (by_even & is_even, ordered(mine1, mine2, start)),
+            (by_even, ordered(x1, x2, start)),
+            (plane == 1, simple(h1, clipped)),
+            (plane == 2, simple(h2, clipped)),
+            (None, simple(h3, clipped)),
+        ]
+    )
+    own_late = pick(
+        [
+            (plane == 0, local(range(2 + 2 * cut, 2 * n_cols, 2))),
+            (by_even & is_even, ordered(mine1, mine2, late)),
+            (by_even, ordered(x1, x2, late)),
+            (plane == 1, simple(h2, range(cut))),
+            (plane == 2, simple(h3, range(cut))),
+            (None, simple(h4, range(cut))),
+        ]
+    )
+
+    def rows(own):
+        return own, route(own, TWINS), second_cols, second_twin
 
     def place(by):
         flags = [p, p % 2, q, jnp.where(by, home, core == 0), by, home, core]
         return jnp.stack([x.astype(jnp.int32) for x in flags])
 
     noise_rows = noise.reshape(-1, 1, NB)
-    rows_1 = rows(own_1, slice(0, n_cols))
-    rows_2 = rows(own_2, slice(0, 1 + cut))
-    cols = (col_mine.reshape(-1, NB), col_given.reshape(-1, NB))
+    rows_early, rows_late = rows(own_early), rows(own_late)
+    args = (factored, 4, N_COL)
     done = update(
-        place(by_odd),
-        lambda r: 2 * r + 1,
-        n_cols,
+        place(by_even),
+        lambda r: 2 * r,
+        1 + cut,
         kernel,
         noise_rows,
-        rows_1,
-        factored,
-        4,
-        N_COL,
-        cols=cols,
-    )
-    h4 = after(h4, done[1])
-    own_3 = jnp.where(
-        plane == 0,
-        even(late),
-        jnp.where(
-            by_even,
-            first_cols[late],
-            jnp.where(plane == 1, h2, jnp.where(plane == 2, h3, h4)),
-        ),
-    )
-    rows_3 = rows(own_3, late)
+        rows_early,
+        *args,
+        cols=(mine1, mine2, x1, x2),
+    )
+    mine_down1, mine_down2, other_down1, other_down2, _ = lax.optimization_barrier(
+        (mine_down1, mine_down2, other_down1, other_down2, done[1])
+    )
+    own_odd = pick(
+        [
+            (plane == 0, local(range(1, 2 * n_cols, 2))),
+            (by_odd & is_even, ordered(mine1, mine2, everything)),
+            (by_odd, ordered(x1, x2, everything)),
+            (by_even, simple(risen, range(n_cols))),
+            (plane == 3, simple(h1, clipped) + simple(h2, range(cut))),
+            (home, ordered(mine_down1, mine_down2, everything)),
+            (None, ordered(other_down1, other_down2, everything)),
+        ]
+    )
+    rows_odd = rows(own_odd)
     done = update(
-        place(by_even), lambda r: 2 * r, 1 + cut, kernel, noise_rows, rows_2, factored, 4, N_COL, done=done
-    )
-    return update(
         place(by_even),
         lambda r: 2 * (1 + cut + r),
         cut,
         kernel,
         noise_rows,
-        rows_3,
-        factored,
-        4,
-        N_COL,
+        rows_late,
+        *args,
+        first_block=1 + cut,
         done=done,
+    )
+    return update(
+        place(by_odd), lambda r: 2 * r + 1, n_cols, kernel, noise_rows, rows_odd, *args, done=done
     )[0]
 
 

time: 141 us -> 149 us (1.057)
  the two profiles are of different devices: /device:TPU:0 before, /device:TPU:31 now
where the time goes in v2:
time: 149 us; the launch traced here: 148 us
  Pallas kernels  48.3 us (32%)
  waiting for transfers between devices  38.3 us (26%)
  starting transfers between devices  37.8 us (25%)
  local copies, waits for them, and re-layouts  16.8 us (11%)
  other arithmetic  5.89 us (4%)
    ppermute x23, waiting for transfers between devices, route(): lax.ppermute(x, BOTH, [(a[0] * N_COL + a[1], b[0] * N_COL + b[1]) for a,...  38.3 us
    ppermute x23, starting transfers between devices, route(): lax.ppermute(x, BOTH, [(a[0] * N_COL + a[1], b[0] * N_COL + b[1]) for a,...  37.8 us
    pallas_call x3, Pallas kernels, update(): pl.pallas_call(functools.partial(update_kernel, n_row, n_col, step_of, co...  22.7 us
    pallas_call x4, Pallas kernels, factor_call(): pl.pallas_call(fn, out_shape=[jax.ShapeDtypeStruct(s, jnp.float32) for s...  16.9 us
    unnamed x62, local copies, waits for them, and re-layouts  9.7 us
    pallas_call x4, Pallas kernels, pick(): pl.pallas_call(functools.partial(pick_kernel, lists), in_specs=[pl.BlockS...  8.74 us
  transfers between devices with their start and end apart: 23, of which 5 were waited for; matrix products, arithmetic and copies ran while one was open for 8% of the time, Pallas kernels for 24%

profile of v2, /device:TPU:31, one launch (start us, length us, event | category | flops | bytes accessed | tf_op | source)
XLA Modules:
  0.0 148.2 jit_solution(17072420339782357377)
XLA Ops:
  0.0 0.7 slice.129
  0.7 1.0 add_select_fusion
  1.8 0.7 collective-permute-start
  2.5 0.0 slice-start
  2.5 1.3 slice-done
  3.8 1.5 copy.10
  5.3 1.3 fusion.2
  6.5 1.1 fusion.1
  7.7 0.7 collective-permute-start.3
  8.4 2.6 %slice_bitcast_fusion = f32[5,256,256]{2,1,0:T(8,128)} fusion(f32[5,2,256,1280]{3,2,1,0:T(8,128)} %bitcast.93), kind=kLoop, calls=%fused_computation | loop fusion | bytes 2621440 | tf_op jit(solution)/shard_map/squeeze | solution.py:509
  11.0 0.7 collective-permute-start.1
  11.6 1.3 collective-permute-start.5
  12.9 1.0 slice_bitcast_fusion.3
  14.0 0.7 collective-permute-start.2
  14.7 0.1 pad_maximum_fusion
  14.8 1.3 collective-permute-start.4
  16.1 1.7 %collective-permute-start.8 = (f32[5,256,256]{2,1,0:T(8,128)}, f32[5,256,256]{2,1,0:T(8,128)}, u32[]{:S(2)}, u32[]{:S(2)}) collective-permute-start(f32[5,256,256]{2,1,0:T(8,128)} %slice_bitcast_fusion), channel_id=1, source_target_pairs={{16,18},{17,19},{24,26},{25,27}} | collective-permute-start | bytes 3932168 | tf_op jit(solution)/shard_map/ppermute | solution.py:458
  17.8 8.6 %collective-permute-done.5 = f32[2,256,256]{2,1,0:T(8,128)} collective-permute-done((f32[2,256,256]{2,1,0:T(8,128)S(1)}, f32[2,256,256]{2,1,0:T(8,128)}, u32[]{:S(2)}, u32[]{:S(2)}) %collective-permute-start.5) | collective-permute-done | bytes 524320 | tf_op jit(solution)/shard_map/ppermute | solution.py:458
  26.4 1.1 broadcast_select_fusion.1.refs_2_.refs_3_.refs_12_
  27.6 0.1 broadcast_select_fusion.2
  27.7 4.1 %shard_map.28 = (f32[128,128]{1,0:T(8,128)S(1)}, f32[128,128]{1,0:T(8,128)S(1)}, f32[128,128]{1,0:T(8,128)S(1)}, f32[128,128]{1,0:T(8,128)S(1)}) custom-call(f32[3,128,128]{2,1,0:T(8,128)S(1)} %get-tuple-element.40.block), custom_call_target="tpu_custom_call" | custom-call | tf_op jit(solution)/shard_map/pallas_call | solution.py:131
  31.8 0.3 collective-permute-start.6
  32.1 5.2 %collective-permute-start.10 = (f32[2,256,256]{2,1,0:T(8,128)S(1)}, f32[2,256,256]{2,1,0:T(8,128)S(1)}, u32[]{:S(2)}, u32[]{:S(2)}) collective-permute-start(f32[2,256,256]{2,1,0:T(8,128)S(1)} %broadcast_select_fusion.1.refs_2_.refs_3_.refs_12_), channel_id=1, source_target_pairs={{4,2},{13,11},{22,20},{31,29}} | collective-permute-start | bytes 1572872 | tf_op jit(solution)/shard_map/ppermute | solution.py:458
  37.4 1.2 fusion
  38.6 0.9 collective-permute-start.9
  39.5 3.8 %shard_map.29 = (f32[256,256]{1,0:T(8,128)S(1)}, f32[256,256]{1,0:T(8,128)S(1)}) custom-call(f32[128,128]{1,0:T(8,128)S(1)} %get-tuple-element.41.factor, f32[128,128]{1,0:T(8,128)S(1)} %get-tuple-element.42.inverse, f32[128,128]{1,0:T(8,128)S(1)} %get-tuple-element.43.below, f32[128,128]{1,0:T(8,128)S(1)} %get-tuple-element.44.rest), custom_call_target="tpu_custom_call" | custom-call | tf_op jit(solution)/shard_map/pallas_call | solution.py:131
  43.3 5.2 %shard_map.30 = (f32[256,256]{1,0:T(8,128)S(1)}, f32[128,128]{1,0:T(8,128)S(1)}, f32[128,128]{1,0:T(8,128)S(1)}, f32[128,128]{1,0:T(8,128)S(1)}, f32[128,128]{1,0:T(8,128)S(1)}) custom-call(f32[3,128,128]{2,1,0:T(8,128)S(1)} %get-tuple-element.80.side, f32[3,128,128]{2,1,0:T(8,128)S(1)} %get-tuple-element.82.turned, ...), custom_call_target="tpu_custom_call" | custom-call | tf_op jit(solution)/shard_map/pallas_call | solution.py:131
  48.6 0.1 broadcast_select_fusion.refs_1_.refs_2_.refs_13_
  48.7 2.8 %collective-permute-start.11 = (f32[3,256,256]{2,1,0:T(8,128)S(1)}, f32[3,256,256]{2,1,0:T(8,128)}, u32[]{:S(2)}, u32[]{:S(2)}) collective-permute-start(f32[3,256,256]{2,1,0:T(8,128)S(1)} %broadcast_select_fusion.refs_1_.refs_2_.refs_13_), channel_id=1, source_target_pairs={{4,2},{13,11},{22,20},{31,29}} | collective-permute-start | bytes 2359304 | tf_op jit(solution)/shard_map/ppermute | solution.py:458
  51.5 6.8 %collective-permute-start.12 = (f32[2,256,256]{2,1,0:T(8,128)S(1)}, f32[2,256,256]{2,1,0:T(8,128)}, u32[]{:S(2)}, u32[]{:S(2)}) collective-permute-start(f32[2,256,256]{2,1,0:T(8,128)S(1)} %collective-permute-done.6.refs_4_.refs_1_.refs_14_), channel_id=1, source_target_pairs={{4,3},{13,10},{22,21},{31,28}} | collective-permute-start | bytes 1572872 | tf_op jit(solution)/shard_map/ppermute | solution.py:458
  58.2 3.8 %shard_map.33 = (f32[256,256]{1,0:T(8,128)S(1)}, f32[256,256]{1,0:T(8,128)S(1)}) custom-call(f32[128,128]{1,0:T(8,128)S(1)} %get-tuple-element.57.factor, f32[128,128]{1,0:T(8,128)S(1)} %get-tuple-element.58.inverse, f32[128,128]{1,0:T(8,128)S(1)} %get-tuple-element.59.below, f32[128,128]{1,0:T(8,128)S(1)} %get-tuple-element.60.rest), custom_call_target="tpu_custom_call" | custom-call | tf_op jit(solution)/shard_map/pallas_call | solution.py:131
  62.2 0.8 copy-done.25
  63.0 1.4 collective-permute-start.17
  64.4 0.9 slice_select_fusion
  65.3 1.3 collective-permute-start.14
  66.7 11.8 %collective-permute-done.14.refs_7_.refs_4_ = f32[2,256,256]{2,1,0:T(8,128)} collective-permute-done((f32[2,256,256]{2,1,0:T(8,128)}, f32[2,256,256]{2,1,0:T(8,128)}, u32[]{:S(2)}, u32[]{:S(2)}) %collective-permute-start.14) | collective-permute-done | bytes 524320 | tf_op jit(solution)/shard_map/ppermute | solution.py:458
  78.4 1.3 collective-permute-start.18
  79.8 0.0 copy-start.26
  79.8 2.4 %shard_map.32.refs_5_ = f32[5,256,256]{2,1,0:T(8,128)} custom-call(s32[1]{0:T(128)} %bitcast.28.which, f32[3,256,256]{2,1,0:T(8,128)} %copy-done.3, f32[2,256,256]{2,1,0:T(8,128)} %copy-done.7, f32[3,256,256]{2,1,0:T(8,128)} %copy-done, f32[2,256,256]{2,1,0:T(8,128)} %copy-done.5), custom_call_target="tpu_custom_call" | custom-call | tf_op jit(solution)/shard_map/pallas_call | solution.py:340
  82.2 2.4 %collective-permute-start.16 = (f32[5,256,256]{2,1,0:T(8,128)}, f32[5,256,256]{2,1,0:T(8,128)}, u32[]{:S(2)}, u32[]{:S(2)}) collective-permute-start(f32[5,256,256]{2,1,0:T(8,128)} %shard_map.32.refs_5_), channel_id=1, source_target_pairs={{4,5},{13,12},{22,23},{31,30},{18,19},{27,26}} | collective-permute-start | bytes 3932168 | tf_op jit(solution)/shard_map/ppermute | solution.py:458
  84.6 9.0 %collective-permute-done.18 = f32[5,128,128]{2,1,0:T(8,128)S(1)} collective-permute-done((f32[5,128,128]{2,1,0:T(8,128)S(1)}, f32[5,128,128]{2,1,0:T(8,128)S(1)}, u32[]{:S(2)}, u32[]{:S(2)}) %collective-permute-start.18) | collective-permute-done | bytes 327712 | tf_op jit(solution)/shard_map/ppermute | solution.py:458
  93.6 0.8 collective-permute-start.19
  94.5 0.1 stack.134.refs_0_
  94.6 1.3 collective-permute-start.20
  95.9 2.1 %shard_map.31.refs_3_ = f32[3,256,256]{2,1,0:T(8,128)} custom-call(s32[1]{0:T(128)} %bitcast.27.which, f32[2560,1280]{1,0:T(8,128)} %refs_1_.5, f32[3,256,256]{2,1,0:T(8,128)} %copy-done, f32[2,256,256]{2,1,0:T(8,128)} %copy-done.5, f32[3,256,256]{2,1,0:T(8,128)} %copy-done.3, f32[2,256,256]{2,1,0:T(8,128)} %copy-done.7, f32[2,256,256]{2,1,0:T(8,128)} %copy-done.23, ...), custom_call_target="tpu_custom_call" | custom-call | tf_op jit(solution)/shard_map/pallas_call | solution.py:340
  98.0 0.1 collective-permute-start.15
  98.1 5.1 %collective-permute-start.13 = (f32[3,256,256]{2,1,0:T(8,128)S(1)}, f32[3,256,256]{2,1,0:T(8,128)S(1)}, u32[]{:S(2)}, u32[]{:S(2)}) collective-permute-start(f32[3,256,256]{2,1,0:T(8,128)S(1)} %copy-done.4), channel_id=1, source_target_pairs={{4,3},{13,10},{22,21},{31,28}} | collective-permute-start | bytes 2359304 | tf_op jit(solution)/shard_map/ppermute | solution.py:458
  103.5 6.8 %collective-permute-done.20.refs_5_ = f32[2,256,256]{2,1,0:T(8,128)} collective-permute-done((f32[2,256,256]{2,1,0:T(8,128)}, f32[2,256,256]{2,1,0:T(8,128)}, u32[]{:S(2)}, u32[]{:S(2)}) %collective-permute-start.20) | collective-permute-done | bytes 524320 | tf_op jit(solution)/shard_map/ppermute | solution.py:458
  110.5 7.2 %shard_map.34 = (f32[2560,1280]{1,0:T(8,128)}, bf16[512,1280]{1,0:T(8,128)(2,1)S(1)}, bf16[512,1280]{1,0:T(8,128)(2,1)S(1)}) custom-call(s32[7]{0:T(128)S(1)} %stack.134.refs_0_, f32[2560,1280]{1,0:T(8,128)} %refs_1_.5, f32[10,1,256]{2,1,0:T(1,128)S(1)} %reshape.21.refs_2_, f32[3,256,256]{2,1,0:T(8,128)S(1)} %copy-done.15, ...), custom_call_target="tpu_custom_call" | custom-call | flops 3925868544 | bytes 7864320 | tf_op jit(solution)/shard_map/pallas_call | solution.py:288
  117.7 1.1 copy-done.9
  118.7 1.1 copy-done.11
  119.8 0.9 copy-done.24
  120.7 2.4 %shard_map.35.refs_3_ = f32[5,256,256]{2,1,0:T(8,128)} custom-call(s32[1]{0:T(128)} %bitcast.7.which, f32[2560,1280]{1,0:T(8,128)} %refs_1_.5, f32[3,256,256]{2,1,0:T(8,128)} %copy-done, f32[2,256,256]{2,1,0:T(8,128)} %copy-done.5, f32[3,256,256]{2,1,0:T(8,128)} %copy-done.3, f32[2,256,256]{2,1,0:T(8,128)} %copy-done.7, ...), custom_call_target="tpu_custom_call" | custom-call | tf_op jit(solution)/shard_map/pallas_call | solution.py:340
  123.1 0.9 collective-permute-start.21
  124.0 1.8 %shard_map.36.refs_3_ = f32[2,256,256]{2,1,0:T(8,128)} custom-call(s32[1]{0:T(128)} %bitcast.27.which, f32[2560,1280]{1,0:T(8,128)} %refs_1_.5, f32[3,256,256]{2,1,0:T(8,128)} %copy-done, f32[3,256,256]{2,1,0:T(8,128)} %copy-done.3, f32[2,256,256]{2,1,0:T(8,128)} %copy-done.22, f32[2,256,256]{2,1,0:T(8,128)} %collective-permute-done.14.refs_7_.refs_4_, ...), custom_call_target="tpu_custom_call" | custom-call | tf_op jit(solution)/shard_map/pallas_call | solution.py:340
  125.8 0.2 collective-permute-start.22
  126.1 0.1 stack.122.refs_0_
  126.1 2.0 %collective-permute-done.22.refs_4_ = f32[2,256,256]{2,1,0:T(8,128)} collective-permute-done((f32[2,256,256]{2,1,0:T(8,128)}, f32[2,256,256]{2,1,0:T(8,128)}, u32[]{:S(2)}, u32[]{:S(2)}) %collective-permute-start.22) | collective-permute-done | bytes 524320 | tf_op jit(solution)/shard_map/ppermute | solution.py:458
  128.2 1.3 copy-done.12
  129.5 0.9 copy-done.17
  130.4 0.9 copy-done.19
  131.4 1.0 copy-done.21
  132.4 5.9 %shard_map.37.refs_14_ = f32[2560,1280]{1,0:T(8,128)} custom-call(s32[7]{0:T(128)S(1)} %stack.134.refs_0_, f32[2560,1280]{1,0:T(8,128)} %refs_1_.5, f32[10,1,256]{2,1,0:T(1,128)S(1)} %reshape.21.refs_2_, f32[2,256,256]{2,1,0:T(8,128)S(1)} %copy-done.21, f32[2,256,256]{2,1,0:T(8,128)} %collective-permute-done.22.refs_4_, ...), custom_call_target="tpu_custom_call", output_to_operand_aliasing={{}: (14, {})} | custom-call | flops 1610612736 | bytes 5242880 | tf_op jit(solution)/shard_map/pallas_call | solution.py:288
  138.4 9.6 %shard_map.38 = f32[2560,1280]{1,0:T(8,128)} custom-call(s32[7]{0:T(128)S(1)} %stack.122.refs_0_, f32[2560,1280]{1,0:T(8,128)} %refs_1_.5, f32[10,1,256]{2,1,0:T(1,128)S(1)} %reshape.21.refs_2_, f32[5,256,256]{2,1,0:T(8,128)S(1)} %copy-done.14, f32[5,256,256]{2,1,0:T(8,128)} %collective-permute-done.21.refs_4_, ...), custom_call_target="tpu_custom_call", output_to_operand_aliasing={{}: (14, {})} | custom-call | flops 4026531840 | bytes 13107200 | tf_op jit(solution)/shard_map/pallas_call | solution.py:288
  (88 shorter events, 0.7 us)
Async XLA Ops:
  1.8 9.1 %collective-permute-start = (f32[3,128,128]{2,1,0:T(8,128)S(1)}, f32[3,128,128]{2,1,0:T(8,128)S(1)}, u32[]{:S(2)}, u32[]{:S(2)}) collective-permute-start(f32[3,128,128]{2,1,0:T(8,128)S(1)} %pad_maximum_fusion.2), channel_id=1, source_target_pairs={{0,16},{1,17},{8,24},{9,25}} | collective-permute-start | bytes 589832 | tf_op jit(solution)/shard_map/ppermute | solution.py:458
  2.5 1.3 slice-start
  7.7 20.0 %collective-permute-start.3 = (f32[2,256,256]{2,1,0:T(8,128)S(1)}, f32[2,256,256]{2,1,0:T(8,128)S(1)}, u32[]{:S(2)}, u32[]{:S(2)}) collective-permute-start(f32[2,256,256]{2,1,0:T(8,128)S(1)} %fusion.1), channel_id=1, source_target_pairs={{0,2},{1,3},{8,10},{9,11},{4,6},{12,7},{5,14},{13,15}} | collective-permute-start | bytes 1572872 | tf_op jit(solution)/shard_map/ppermute | solution.py:458
  11.0 3.0 %collective-permute-start.1 = (f32[3,128,128]{2,1,0:T(8,128)S(1)}, f32[3,128,128]{2,1,0:T(8,128)S(1)}, u32[]{:S(2)}, u32[]{:S(2)}) collective-permute-start(f32[3,128,128]{2,1,0:T(8,128)S(1)} %broadcast_select_fusion.9), channel_id=1, source_target_pairs={{0,8},{1,9},{8,0},{9,1},{16,24},{17,25},{24,16},{25,17}} | collective-permute-start | bytes 589832 | tf_op jit(solution)/shard_map/ppermute | solution.py:458
  11.6 14.8 %collective-permute-start.5 = (f32[2,256,256]{2,1,0:T(8,128)S(1)}, f32[2,256,256]{2,1,0:T(8,128)}, u32[]{:S(2)}, u32[]{:S(2)}) collective-permute-start(f32[2,256,256]{2,1,0:T(8,128)S(1)} %bitcast.98), channel_id=1, source_target_pairs={{0,16},{1,17},{2,18},{3,19},{4,20},{5,21},{6,22},{7,23},{8,24},{9,... | collective-permute-start | bytes 1572872 | tf_op jit(solution)/shard_map/ppermute | solution.py:458
  14.0 13.5 %collective-permute-start.2 = (f32[2,3,128,128]{3,2,1,0:T(8,128)S(1)}, f32[2,3,128,128]{3,2,1,0:T(8,128)S(1)}, u32[]{:S(2)}, u32[]{:S(2)}) collective-permute-start(f32[2,3,128,128]{3,2,1,0:T(8,128)S(1)} %pad_maximum_fusion.1), channel_id=1, source_target_pairs={{0,1},{1,0},{8,9},{9,8},{16,17},{17,16},{24,25},{25,24}} | collective-permute-start | bytes 1179656 | tf_op jit(solution)/shard_map/ppermute | solution.py:458
  14.8 33.8 %collective-permute-start.4 = (f32[3,256,256]{2,1,0:T(8,128)S(1)}, f32[3,256,256]{2,1,0:T(8,128)S(1)}, u32[]{:S(2)}, u32[]{:S(2)}) collective-permute-start(f32[3,256,256]{2,1,0:T(8,128)S(1)} %pad_maximum_fusion), channel_id=1, source_target_pairs={{0,16},{1,17},{2,18},{3,19},{4,20},{5,21},{6,22},{7,23},{8,24},{9,... | collective-permute-start | bytes 2359304 | tf_op jit(solution)/shard_map/ppermute | solution.py:458
  16.1 46.9 %collective-permute-start.8 = (f32[5,256,256]{2,1,0:T(8,128)}, f32[5,256,256]{2,1,0:T(8,128)}, u32[]{:S(2)}, u32[]{:S(2)}) collective-permute-start(f32[5,256,256]{2,1,0:T(8,128)} %slice_bitcast_fusion), channel_id=1, source_target_pairs={{16,18},{17,19},{24,26},{25,27}} | collective-permute-start | bytes 3932168 | tf_op jit(solution)/shard_map/ppermute | solution.py:458
  27.5 9.8 %copy-start.5 = (f32[2,256,256]{2,1,0:T(8,128)}, f32[2,256,256]{2,1,0:T(8,128)S(1)}, u32[]{:S(2)}) copy-start(f32[2,256,256]{2,1,0:T(8,128)S(1)} %broadcast_select_fusion.1.refs_2_.refs_3_.refs_12_) | copy-start | bytes 1572868
  27.7 10.9 %copy-start.23 = (f32[2,256,256]{2,1,0:T(8,128)}, f32[2,256,256]{2,1,0:T(8,128)S(1)}, u32[]{:S(2)}) copy-start(f32[2,256,256]{2,1,0:T(8,128)S(1)} %collective-permute-done.3.refs_5_.refs_6_) | copy-start | bytes 1572868
  31.8 19.7 %collective-permute-start.6 = (f32[2,256,256]{2,1,0:T(8,128)S(1)}, f32[2,256,256]{2,1,0:T(8,128)S(1)}, u32[]{:S(2)}, u32[]{:S(2)}) collective-permute-start(f32[2,256,256]{2,1,0:T(8,128)S(1)} %broadcast_select_fusion.1.refs_2_.refs_3_.refs_12_), channel_id=1, source_target_pairs={{0,8},{1,9},{2,10},{3,11},{4,12},{5,13},{6,14},{7,15},{8,0},{9,1},... | collective-permute-start | bytes 1572872 | tf_op jit(solution)/shard_map/ppermute | solution.py:458
  32.1 30.0 %collective-permute-start.10 = (f32[2,256,256]{2,1,0:T(8,128)S(1)}, f32[2,256,256]{2,1,0:T(8,128)S(1)}, u32[]{:S(2)}, u32[]{:S(2)}) collective-permute-start(f32[2,256,256]{2,1,0:T(8,128)S(1)} %broadcast_select_fusion.1.refs_2_.refs_3_.refs_12_), channel_id=1, source_target_pairs={{4,2},{13,11},{22,20},{31,29}} | collective-permute-start | bytes 1572872 | tf_op jit(solution)/shard_map/ppermute | solution.py:458
  38.6 12.9 %collective-permute-start.9 = (f32[2,256,256]{2,1,0:T(8,128)S(1)}, f32[2,256,256]{2,1,0:T(8,128)S(1)}, u32[]{:S(2)}, u32[]{:S(2)}) collective-permute-start(f32[2,256,256]{2,1,0:T(8,128)S(1)} %fusion), channel_id=1, source_target_pairs={{0,2},{1,3},{8,10},{9,11},{2,4},{3,5},{10,12},{11,13},{18,20},{26,... | collective-permute-start | bytes 1572872 | tf_op jit(solution)/shard_map/ppermute | solution.py:458
  43.3 67.1 %copy-start.16 = (f32[256,256]{1,0:T(8,128)}, f32[256,256]{1,0:T(8,128)S(1)}, u32[]{:S(2)}) copy-start(f32[256,256]{1,0:T(8,128)S(1)} %get-tuple-element.55.refs_7_) | copy-start | bytes 786436
  48.7 16.6 %copy-start = (f32[3,256,256]{2,1,0:T(8,128)}, f32[3,256,256]{2,1,0:T(8,128)S(1)}, u32[]{:S(2)}) copy-start(f32[3,256,256]{2,1,0:T(8,128)S(1)} %broadcast_select_fusion.refs_1_.refs_2_.refs_13_) | copy-start | bytes 2359300
  48.7 29.8 %collective-permute-start.11 = (f32[3,256,256]{2,1,0:T(8,128)S(1)}, f32[3,256,256]{2,1,0:T(8,128)}, u32[]{:S(2)}, u32[]{:S(2)}) collective-permute-start(f32[3,256,256]{2,1,0:T(8,128)S(1)} %broadcast_select_fusion.refs_1_.refs_2_.refs_13_), channel_id=1, source_target_pairs={{4,2},{13,11},{22,20},{31,29}} | collective-permute-start | bytes 2359304 | tf_op jit(solution)/shard_map/ppermute | solution.py:458
  51.5 13.8 %copy-start.7 = (f32[2,256,256]{2,1,0:T(8,128)}, f32[2,256,256]{2,1,0:T(8,128)S(1)}, u32[]{:S(2)}) copy-start(f32[2,256,256]{2,1,0:T(8,128)S(1)} %collective-permute-done.6.refs_4_.refs_1_.refs_14_) | copy-start | bytes 1572868
  51.5 27.0 %collective-permute-start.7 = (f32[3,256,256]{2,1,0:T(8,128)S(1)}, f32[3,256,256]{2,1,0:T(8,128)S(1)}, u32[]{:S(2)}, u32[]{:S(2)}) collective-permute-start(f32[3,256,256]{2,1,0:T(8,128)S(1)} %broadcast_select_fusion.refs_1_.refs_2_.refs_13_), channel_id=1, source_target_pairs={{0,8},{1,9},{2,10},{3,11},{4,12},{5,13},{6,14},{7,15},{8,0},{9,1},... | collective-permute-start | bytes 2359304 | tf_op jit(solution)/shard_map/ppermute | solution.py:458
  51.5 13.8 %copy-start.22 = (f32[2,256,256]{2,1,0:T(8,128)}, f32[2,256,256]{2,1,0:T(8,128)S(1)}, u32[]{:S(2)}) copy-start(f32[2,256,256]{2,1,0:T(8,128)S(1)} %collective-permute-done.9.refs_6_.refs_7_.refs_3_) | copy-start | bytes 1572868
  51.5 15.2 %collective-permute-start.12 = (f32[2,256,256]{2,1,0:T(8,128)S(1)}, f32[2,256,256]{2,1,0:T(8,128)}, u32[]{:S(2)}, u32[]{:S(2)}) collective-permute-start(f32[2,256,256]{2,1,0:T(8,128)S(1)} %collective-permute-done.6.refs_4_.refs_1_.refs_14_), channel_id=1, source_target_pairs={{4,3},{13,10},{22,21},{31,28}} | collective-permute-start | bytes 1572872 | tf_op jit(solution)/shard_map/ppermute | solution.py:458
  62.1 48.3 %copy-start.18 = (f32[256,256]{1,0:T(8,128)}, f32[256,256]{1,0:T(8,128)S(1)}, u32[]{:S(2)}) copy-start(f32[256,256]{1,0:T(8,128)S(1)} %get-tuple-element.64.refs_10_) | copy-start | bytes 786436
  62.2 0.8 copy-start.25
  63.0 3.6 %collective-permute-start.17 = (f32[5,128,128]{2,1,0:T(8,128)S(1)}, f32[5,128,128]{2,1,0:T(8,128)}, u32[]{:S(2)}, u32[]{:S(2)}) collective-permute-start(f32[5,128,128]{2,1,0:T(8,128)S(1)} %broadcast_select_fusion.8), channel_id=1, source_target_pairs={{0,4},{1,5},{8,12},{9,13},{16,20},{17,21},{24,28},{25,29}} | collective-permute-start | bytes 983048 | tf_op jit(solution)/shard_map/ppermute | solution.py:458
  65.3 13.1 %collective-permute-start.14 = (f32[2,256,256]{2,1,0:T(8,128)}, f32[2,256,256]{2,1,0:T(8,128)}, u32[]{:S(2)}, u32[]{:S(2)}) collective-permute-start(f32[2,256,256]{2,1,0:T(8,128)} %slice_select_fusion), channel_id=1, source_target_pairs={{2,4},{3,5},{10,12},{11,13},{18,20},{26,21},{19,28},{27,29},{4,6},... | collective-permute-start | bytes 1572872 | tf_op jit(solution)/shard_map/ppermute | solution.py:458
  78.4 1.3 copy-start.3
  78.4 15.1 %collective-permute-start.18 = (f32[5,128,128]{2,1,0:T(8,128)S(1)}, f32[5,128,128]{2,1,0:T(8,128)S(1)}, u32[]{:S(2)}, u32[]{:S(2)}) collective-permute-start(f32[5,128,128]{2,1,0:T(8,128)S(1)} %broadcast_select_fusion.4), channel_id=1, source_target_pairs={{0,2},{1,3},{4,6},{5,7},{8,10},{9,11},{12,14},{13,15},{16,18},{17,... | collective-permute-start | bytes 983048 | tf_op jit(solution)/shard_map/ppermute | solution.py:458
  79.8 14.7 %copy-start.26 = (f32[2560]{0:T(1024)S(1)}, f32[2560]{0:T(1024)}, u32[]{:S(2)}) copy-start(f32[2560]{0:T(1024)} %param.3) | copy-start | bytes 30724
  82.2 28.2 %collective-permute-start.16 = (f32[5,256,256]{2,1,0:T(8,128)}, f32[5,256,256]{2,1,0:T(8,128)}, u32[]{:S(2)}, u32[]{:S(2)}) collective-permute-start(f32[5,256,256]{2,1,0:T(8,128)} %shard_map.32.refs_5_), channel_id=1, source_target_pairs={{4,5},{13,12},{22,23},{31,30},{18,19},{27,26}} | collective-permute-start | bytes 3932168 | tf_op jit(solution)/shard_map/ppermute | solution.py:458
  93.6 9.7 %collective-permute-start.19 = (f32[5,128,128]{2,1,0:T(8,128)S(1)}, f32[5,128,128]{2,1,0:T(8,128)S(1)}, u32[]{:S(2)}, u32[]{:S(2)}) collective-permute-start(f32[5,128,128]{2,1,0:T(8,128)S(1)} %broadcast_select_fusion.5), channel_id=1, source_target_pairs={{0,1},{1,0},{2,3},{3,2},{4,5},{5,4},{6,7},{7,6},{8,9},{9,8},{10,11... | collective-permute-start | bytes 983048 | tf_op jit(solution)/shard_map/ppermute | solution.py:458
  94.6 15.7 %collective-permute-start.20 = (f32[2,256,256]{2,1,0:T(8,128)}, f32[2,256,256]{2,1,0:T(8,128)}, u32[]{:S(2)}, u32[]{:S(2)}) collective-permute-start(f32[2,256,256]{2,1,0:T(8,128)} %collective-permute-done.14.refs_7_.refs_4_), channel_id=1, source_target_pairs={{4,6},{5,7},{12,14},{13,15},{20,22},{21,23},{28,30},{29,31}} | collective-permute-start | bytes 1572872 | tf_op jit(solution)/shard_map/ppermute | solution.py:458
  95.9 2.3 %copy-start.4 = (f32[3,256,256]{2,1,0:T(8,128)S(1)}, f32[3,256,256]{2,1,0:T(8,128)}, u32[]{:S(2)}) copy-start(f32[3,256,256]{2,1,0:T(8,128)} %copy-done.3) | copy-start | bytes 2359300
  98.0 12.3 %collective-permute-start.15 = (f32[3,256,256]{2,1,0:T(8,128)}, f32[3,256,256]{2,1,0:T(8,128)S(1)}, u32[]{:S(2)}, u32[]{:S(2)}) collective-permute-start(f32[3,256,256]{2,1,0:T(8,128)} %shard_map.31.refs_3_), channel_id=1, source_target_pairs={{0,1},{1,0},{2,3},{3,2},{4,5},{5,4},{6,7},{7,6},{8,9},{9,8},{10,11... | collective-permute-start | bytes 2359304 | tf_op jit(solution)/shard_map/ppermute | solution.py:458
  98.1 21.7 %collective-permute-start.13 = (f32[3,256,256]{2,1,0:T(8,128)S(1)}, f32[3,256,256]{2,1,0:T(8,128)S(1)}, u32[]{:S(2)}, u32[]{:S(2)}) collective-permute-start(f32[3,256,256]{2,1,0:T(8,128)S(1)} %copy-done.4), channel_id=1, source_target_pairs={{4,3},{13,10},{22,21},{31,28}} | collective-permute-start | bytes 2359304 | tf_op jit(solution)/shard_map/ppermute | solution.py:458
  103.3 7.1 %copy-start.8 = (f32[2,256,256]{2,1,0:T(8,128)S(1)}, f32[2,256,256]{2,1,0:T(8,128)}, u32[]{:S(2)}) copy-start(f32[2,256,256]{2,1,0:T(8,128)} %copy-done.7) | copy-start | bytes 1572868
  103.3 7.1 %copy-start.15 = (f32[3,256,256]{2,1,0:T(8,128)S(1)}, f32[3,256,256]{2,1,0:T(8,128)}, u32[]{:S(2)}) copy-start(f32[3,256,256]{2,1,0:T(8,128)} %shard_map.31.refs_3_) | copy-start | bytes 2359300
  103.4 7.1 %copy-start.1 = (f32[3,256,256]{2,1,0:T(8,128)S(1)}, f32[3,256,256]{2,1,0:T(8,128)}, u32[]{:S(2)}) copy-start(f32[3,256,256]{2,1,0:T(8,128)} %copy-done) | copy-start | bytes 2359300
  103.4 7.1 %copy-start.2 = (f32[5,256,256]{2,1,0:T(8,128)S(1)}, f32[5,256,256]{2,1,0:T(8,128)}, u32[]{:S(2)}) copy-start(f32[5,256,256]{2,1,0:T(8,128)} %shard_map.32.refs_5_) | copy-start | bytes 3932164
  103.4 7.0 %copy-start.6 = (f32[2,256,256]{2,1,0:T(8,128)S(1)}, f32[2,256,256]{2,1,0:T(8,128)}, u32[]{:S(2)}) copy-start(f32[2,256,256]{2,1,0:T(8,128)} %copy-done.5) | copy-start | bytes 1572868
  117.7 1.1 copy-start.9
  118.7 1.1 copy-start.11
  119.8 0.9 copy-start.24
  123.1 5.1 %copy-start.10 = (bf16[512,1280]{1,0:T(8,128)(2,1)S(1)}, bf16[512,1280]{1,0:T(8,128)(2,1)}, u32[]{:S(2)}) copy-start(bf16[512,1280]{1,0:T(8,128)(2,1)} %copy-done.9) | copy-start | bytes 3932164
  123.1 15.2 %collective-permute-start.21 = (f32[5,256,256]{2,1,0:T(8,128)}, f32[5,256,256]{2,1,0:T(8,128)}, u32[]{:S(2)}, u32[]{:S(2)}) collective-permute-start(f32[5,256,256]{2,1,0:T(8,128)} %shard_map.35.refs_3_), channel_id=1, source_target_pairs={{0,1},{1,0},{2,3},{3,2},{4,5},{5,4},{6,7},{7,6},{8,9},{9,8},{10,11... | collective-permute-start | bytes 3932168 | tf_op jit(solution)/shard_map/ppermute | solution.py:458
  125.8 2.3 %collective-permute-start.22 = (f32[2,256,256]{2,1,0:T(8,128)}, f32[2,256,256]{2,1,0:T(8,128)}, u32[]{:S(2)}, u32[]{:S(2)}) collective-permute-start(f32[2,256,256]{2,1,0:T(8,128)} %shard_map.36.refs_3_), channel_id=1, source_target_pairs={{0,1},{1,0},{2,3},{3,2},{4,5},{5,4},{6,7},{7,6},{8,9},{9,8},{10,11... | collective-permute-start | bytes 1572872 | tf_op jit(solution)/shard_map/ppermute | solution.py:458
  128.2 1.3 copy-start.12
  129.5 0.9 copy-start.17
  130.4 0.9 copy-start.19
  131.4 1.0 copy-start.21
  132.4 5.9 %copy-start.13 = (bf16[512,1280]{1,0:T(8,128)(2,1)S(1)}, bf16[512,1280]{1,0:T(8,128)(2,1)}, u32[]{:S(2)}) copy-start(bf16[512,1280]{1,0:T(8,128)(2,1)} %copy-done.11) | copy-start | bytes 3932164
  132.4 5.9 %copy-start.14 = (f32[5,256,256]{2,1,0:T(8,128)S(1)}, f32[5,256,256]{2,1,0:T(8,128)}, u32[]{:S(2)}) copy-start(f32[5,256,256]{2,1,0:T(8,128)} %shard_map.35.refs_3_) | copy-start | bytes 3932164
  132.4 5.9 %copy-start.20 = (f32[256,256]{1,0:T(8,128)S(1)}, f32[256,256]{1,0:T(8,128)}, u32[]{:S(2)}) copy-start(f32[256,256]{1,0:T(8,128)} %copy-done.18) | copy-start | bytes 786436

commit v3 on v2

--- a/solution.py
+++ b/solution.py
@@ -9,6 +9,9 @@
 NB = 256
 HB = 128
 HIGHEST = lax.Precision.HIGHEST
+GRANT = 8 * 2**20
+UPDATE_GRANT = 44 * 2**20
+PICK_GRANT = 44 * 2**20
 
 
 def dot_nt(a, b):
@@ -126,7 +129,7 @@
     whole_inverse[HB:, HB:] = lower_inv[...]
 
 
-def factor_call(fn, args, outs, extra=()):
+def factor_call(fn, args, outs, extra=(), flops=0):
     half = pltpu.VMEM((HB, HB), jnp.float32)
     return pl.pallas_call(
         fn,
@@ -139,8 +142,8 @@
             half,
             pltpu.VMEM((64, HB), jnp.float32),
         ],
-        compiler_params=pltpu.CompilerParams(vmem_limit_bytes=32 * 2**20),
-        cost_estimate=pl.CostEstimate(flops=0, bytes_accessed=0, transcendentals=0),
+        compiler_params=pltpu.CompilerParams(vmem_limit_bytes=GRANT),
+        cost_estimate=pl.CostEstimate(flops=flops, bytes_accessed=0, transcendentals=0),
     )(*args)
 
 
@@ -300,7 +303,7 @@
             pltpu.SemaphoreType.DMA((count,)),
         ],
         input_output_aliases={} if done is None else {14: 0},
-        compiler_params=pltpu.CompilerParams(vmem_limit_bytes=40 * 2**20),
+        compiler_params=pltpu.CompilerParams(vmem_limit_bytes=UPDATE_GRANT),
         cost_estimate=pl.CostEstimate(
             flops=flops, bytes_accessed=count * NB * cols_local * 8, transcendentals=0
         ),
@@ -344,6 +347,7 @@
         out_specs=pl.BlockSpec(memory_space=pltpu.VMEM),
         out_shape=jax.ShapeDtypeStruct((count, NB, NB), jnp.float32),
         scratch_shapes=[pltpu.SemaphoreType.DMA((count,))],
+        compiler_params=pltpu.CompilerParams(vmem_limit_bytes=PICK_GRANT),
         cost_estimate=pl.CostEstimate(flops=0, bytes_accessed=0, transcendentals=0),
     )(which.astype(jnp.int32).reshape(1), *sources)
 
@@ -352,17 +356,21 @@
     return factor_call(start_kernel, [corner], QUARTERS)
 
 
-def finish_factor(part, side, turned, next_corner, before_first=(), before_last=()):
+def finish_factor(
+    part, side, turned, next_corner, before_first=(), before_next=(), before_last=()
+):
     part = [after(part[0], *before_first), *part[1:]]
     first_factor, first_inverse = factor_call(finish_kernel, part, [(NB, NB)] * 2)
     cross, *part = factor_call(
         next_kernel,
-        [side, turned, next_corner, first_inverse],
+        [after(side, *before_next), turned, next_corner, first_inverse],
         [(NB, NB)] + QUARTERS,
         [pltpu.VMEM((3, HB, HB), jnp.float32)],
     )
     part = [after(part[0], *before_last), *part[1:]]
-    second_factor, second_inverse = factor_call(finish_kernel, part, [(NB, NB)] * 2)
+    second_factor, second_inverse = factor_call(
+        finish_kernel, part, [(NB, NB)] * 2, flops=5 * 10**9
+    )
     return first_factor, first_inverse, cross, second_factor, second_inverse
 
 
@@ -483,7 +491,7 @@
         square(top[0], zero, top[1], top[2]),
         square(top[3], top[4], low[0], low[1]),
         square(low[2], zero, low[3], low[4]),
-    )
+    ), z
 
 
 TWINS = [((r, c), (r, c ^ 1)) for r in range(4) for c in range(N_COL)]
@@ -521,7 +529,7 @@
     corner = low_part(jnp.where(p == core, corner + head_noise(noise), corner))
 
     got = route(corner, [((r, c), (r + 2, c)) for r in (0, 1) for c in (0, 1)])
-    y1 = route(after(middle, got), along_y)
+    y1 = route(middle, along_y)
     h1 = route(jnp.where(plane == 0, even(early), middle), up(0, low) + lift)
     here = jnp.where(low_line, corner, got)
     lead_x = route(here, [((r, c), (r ^ 1, c)) for r in range(4) for c in (0, 1)])
@@ -529,11 +537,11 @@
     lead = jnp.stack([jnp.where(is_even, here, lead_x), jnp.where(is_even, lead_x, here)])
     lead_twin = route(lead, [((r, c), (r, c ^ 1)) for r in range(4) for c in (0, 1)])
     corner, *rest = arrange(lead, lead_twin, core)
-    begun = start_factor(after(corner, h1))
-
-    others = after(others, lead_x)
+    begun = start_factor(corner)
+
+    others = after(others, lead_twin)
     y2 = route(others, along_y)
-    mine1 = after(jnp.where(low_line, after(middle, lead_x), y1), begun[0])
+    mine1 = jnp.where(low_line, after(middle, begun[0]), after(y1, begun[0]))
     x1 = route(mine1, along_x)
 
     h2 = route(
@@ -548,23 +556,23 @@
     down = [(at, (r, at[1] - 2)) for r, at in homes.items()]
     down_other = [(at, (r, (at[1] - 2) ^ 1)) for r, at in homes.items()]
     mine_down1 = route(mine1, down)
-    risen = route(after(odd(slice(0, n_cols)), lead_x), up(0, high))
-    factored = finish_factor(begun, *rest, before_last=(x1, h2, y2))
-    cross = factored[2]
-    mine2 = jnp.where(low_line, after(others, cross), y2)
+    risen = route(after(odd(slice(0, n_cols)), lead_twin), up(0, high))
+    mine2 = jnp.where(low_line, others, y2)
     x2 = route(after(mine2, x1), along_x)
-    mine_down2 = route(mine2, down)
-    other_down1 = route(after(x1, cross), down_other)
-    other_down2 = route(x2, down_other)
-    h2 = after(h2, cross)
     h3 = route(
         jnp.where((plane == 1) & ~low_line, mine2[1:], h2), up(1, low) + side + up(2, low + high)
     )
-    h4 = route(h3, up(2, low + high))
-    inverses = spread_inverses(
-        factored, (h2, risen, mine_down1), (x2, h3, mine_down2, other_down1), plane, core
-    )
-    factored = (factored[0], inverses[0], inverses[1], factored[3], after(inverses[2], h4))
+    factored = finish_factor(
+        begun, *rest, before_first=(h1,), before_next=(y2, risen), before_last=(x1, h2, x2)
+    )
+    mine_down2 = route(after(mine2, factored[2]), down)
+    other_down1 = route(after(x1, factored[2]), down_other)
+    other_down2 = route(x2, down_other)
+    h4 = route(after(h3, factored[2]), up(2, low + high))
+    inverses, spread = spread_inverses(
+        factored, (h3, mine_down1), (mine_down2, other_down1, h4), plane, core
+    )
+    factored = (factored[0], inverses[0], inverses[1], factored[3], inverses[2])
 
     by_odd = (low_line & (plane == 2)) | (~low_line & (plane == 3))
     by_even = ~low_line & (plane == 1)
@@ -586,27 +594,6 @@
     col_homes = [(at, (at[0], at[1] ^ 1)) for at in (*homes.values(), (2, 2), (3, 3))]
     second_twin = route(second_cols, col_homes)
     clipped = [max(c - 1, 0) for c in range(1 + cut)]
-    own_early = pick(
-        [
-            (plane == 0, local(range(0, 2 + 2 * cut, 2))),
-            (by_even & is_even, ordered(mine1, mine2, start)),
-            (by_even, ordered(x1, x2, start)),
-            (plane == 1, simple(h1, clipped)),
-            (plane == 2, simple(h2, clipped)),
-            (None, simple(h3, clipped)),
-        ]
-    )
-    own_late = pick(
-        [
-            (plane == 0, local(range(2 + 2 * cut, 2 * n_cols, 2))),
-            (by_even & is_even, ordered(mine1, mine2, late)),
-            (by_even, ordered(x1, x2, late)),
-            (plane == 1, simple(h2, range(cut))),
-            (plane == 2, simple(h3, range(cut))),
-            (None, simple(h4, range(cut))),
-        ]
-    )
-
     def rows(own):
         return own, route(own, TWINS), second_cols, second_twin
 
@@ -615,21 +602,6 @@
         return jnp.stack([x.astype(jnp.int32) for x in flags])
 
     noise_rows = noise.reshape(-1, 1, NB)
-    rows_early, rows_late = rows(own_early), rows(own_late)
-    args = (factored, 4, N_COL)
-    done = update(
-        place(by_even),
-        lambda r: 2 * r,
-        1 + cut,
-        kernel,
-        noise_rows,
-        rows_early,
-        *args,
-        cols=(mine1, mine2, x1, x2),
-    )
-    mine_down1, mine_down2, other_down1, other_down2, _ = lax.optimization_barrier(
-        (mine_down1, mine_down2, other_down1, other_down2, done[1])
-    )
     own_odd = pick(
         [
             (plane == 0, local(range(1, 2 * n_cols, 2))),
@@ -641,8 +613,44 @@
             (None, ordered(other_down1, other_down2, everything)),
         ]
     )
-    rows_odd = rows(own_odd)
+    own_early = pick(
+        [
+            (plane == 0, local(range(0, 2 + 2 * cut, 2))),
+            (by_even & is_even, ordered(mine1, mine2, start)),
+            (by_even, ordered(x1, x2, start)),
+            (plane == 1, simple(h1, clipped)),
+            (plane == 2, simple(h2, clipped)),
+            (None, simple(h3, clipped)),
+        ]
+    )
+    rows_early = rows(own_early)
+    args = (factored, 4, N_COL)
     done = update(
+        place(by_odd),
+        lambda r: 2 * r + 1,
+        n_cols,
+        kernel,
+        noise_rows,
+        rows(own_odd),
+        *args,
+        cols=(mine1, mine2, x1, x2),
+    )
+    h4 = after(h4, done[1])
+    own_late = pick(
+        [
+            (plane == 0, local(range(2 + 2 * cut, 2 * n_cols, 2))),
+            (by_even & is_even, ordered(mine1, mine2, late)),
+            (by_even, ordered(x1, x2, late)),
+            (plane == 1, simple(h2, range(cut))),
+            (plane == 2, simple(h3, range(cut))),
+            (None, simple(h4, range(cut))),
+        ]
+    )
+    rows_late = rows(own_late)
+    done = update(
+        place(by_even), lambda r: 2 * r, 1 + cut, kernel, noise_rows, rows_early, *args, done=done
+    )
+    return update(
         place(by_even),
         lambda r: 2 * (1 + cut + r),
         cut,
@@ -652,9 +660,6 @@
         *args,
         first_block=1 + cut,
         done=done,
-    )
-    return update(
-        place(by_odd), lambda r: 2 * r + 1, n_cols, kernel, noise_rows, rows_odd, *args, done=done
     )[0]
 
 

time: 149 us -> 150 us (level)
  the two profiles are of different devices: /device:TPU:31 before, /device:TPU:0 now
where the time goes in v3:
time: 150 us; the launch traced here: 149 us
  Pallas kernels  50.4 us (34%)
  starting transfers between devices  42.4 us (28%)
  waiting for transfers between devices  23.1 us (15%)
  local copies, waits for them, and re-layouts  22.3 us (15%)
  other arithmetic  9.5 us (6%)
    ppermute x23, starting transfers between devices, route(): lax.ppermute(x, BOTH, [(a[0] * N_COL + a[1], b[0] * N_COL + b[1]) for a,...  42.4 us
    pallas_call x3, Pallas kernels, update(): pl.pallas_call(functools.partial(update_kernel, n_row, n_col, step_of, co...  26.6 us
    ppermute x23, waiting for transfers between devices, route(): lax.ppermute(x, BOTH, [(a[0] * N_COL + a[1], b[0] * N_COL + b[1]) for a,...  23.1 us
    pallas_call x4, Pallas kernels, factor_call(): pl.pallas_call(fn, out_shape=[jax.ShapeDtypeStruct(s, jnp.float32) for s...  16.9 us
    unnamed x90, local copies, waits for them, and re-layouts  16.4 us
    pallas_call x4, Pallas kernels, pick(): pl.pallas_call(functools.partial(pick_kernel, lists), in_specs=[pl.BlockS...  7 us
  transfers between devices with their start and end apart: 23, of which 6 were waited for; matrix products, arithmetic and copies ran while one was open for 10% of the time, Pallas kernels for 30%

profile of v3, /device:TPU:0, one launch (start us, length us, event | category | flops | bytes accessed | tf_op | source)
XLA Modules:
  0.0 148.7 jit_solution(15553996881531239232)
XLA Ops:
  0.0 0.7 slice.129
  0.7 1.0 add_select_fusion
  1.8 5.0 %collective-permute-start = (f32[3,128,128]{2,1,0:T(8,128)S(1)}, f32[3,128,128]{2,1,0:T(8,128)S(1)}, u32[]{:S(2)}, u32[]{:S(2)}) collective-permute-start(f32[3,128,128]{2,1,0:T(8,128)S(1)} %pad_maximum_fusion.2), channel_id=1, source_target_pairs={{0,16},{1,17},{8,24},{9,25}} | collective-permute-start | bytes 589832 | tf_op jit(solution)/shard_map/ppermute | solution.py:466
  6.8 1.5 copy.10
  8.3 1.3 fusion.2
  9.6 2.1 %collective-permute-start.4 = (f32[2,256,256]{2,1,0:T(8,128)S(1)}, f32[2,256,256]{2,1,0:T(8,128)}, u32[]{:S(2)}, u32[]{:S(2)}) collective-permute-start(f32[2,256,256]{2,1,0:T(8,128)S(1)} %bitcast.97), channel_id=1, source_target_pairs={{0,16},{1,17},{2,18},{3,19},{4,20},{5,21},{6,22},{7,23},{8,24},{9,... | collective-permute-start | bytes 1572872 | tf_op jit(solution)/shard_map/ppermute | solution.py:466
  11.7 3.4 %collective-permute-start.1 = (f32[3,128,128]{2,1,0:T(8,128)S(1)}, f32[3,128,128]{2,1,0:T(8,128)S(1)}, u32[]{:S(2)}, u32[]{:S(2)}) collective-permute-start(f32[3,128,128]{2,1,0:T(8,128)S(1)} %broadcast_select_fusion.9), channel_id=1, source_target_pairs={{0,8},{1,9},{8,0},{9,1},{16,24},{17,25},{24,16},{25,17}} | collective-permute-start | bytes 589832 | tf_op jit(solution)/shard_map/ppermute | solution.py:466
  15.1 1.9 %fusion = f32[2,256,256]{2,1,0:T(8,128)} fusion(f32[2,256,256]{2,1,0:T(8,128)S(1)} %bitcast.98, f32[5,2,256,1280]{3,2,1,0:T(8,128)} %bitcast.92, pred[]{:T(512)S(6)} %eq.35), kind=kLoop, calls=%fused_computation.4 | loop fusion | flops 131072 | bytes 1572865 | tf_op jit(solution)/shard_map/jit(_where)/select_n | solution.py:533
  17.0 1.3 collective-permute-start.7
  18.3 1.6 %collective-permute-done.1 = f32[3,128,128]{2,1,0:T(8,128)S(1)} collective-permute-done((f32[3,128,128]{2,1,0:T(8,128)S(1)}, f32[3,128,128]{2,1,0:T(8,128)S(1)}, u32[]{:S(2)}, u32[]{:S(2)}) %collective-permute-start.1) | collective-permute-done | bytes 196640 | tf_op jit(solution)/shard_map/ppermute | solution.py:466
  20.0 0.8 pad_maximum_fusion.1
  20.8 1.9 %collective-permute-start.2 = (f32[2,3,128,128]{3,2,1,0:T(8,128)}, f32[2,3,128,128]{3,2,1,0:T(8,128)}, u32[]{:S(2)}, u32[]{:S(2)}) collective-permute-start(f32[2,3,128,128]{3,2,1,0:T(8,128)} %pad_maximum_fusion.1), channel_id=1, source_target_pairs={{0,1},{1,0},{8,9},{9,8},{16,17},{17,16},{24,25},{25,24}} | collective-permute-start | bytes 1179656 | tf_op jit(solution)/shard_map/ppermute | solution.py:466
  22.7 2.6 %slice_bitcast_fusion = f32[5,256,256]{2,1,0:T(8,128)} fusion(f32[5,2,256,1280]{3,2,1,0:T(8,128)} %bitcast.93), kind=kLoop, calls=%fused_computation | loop fusion | bytes 2621440 | tf_op jit(solution)/shard_map/squeeze | solution.py:517
  25.3 1.0 slice_bitcast_fusion.3
  26.3 3.3 %collective-permute-start.3 = (f32[3,256,256]{2,1,0:T(8,128)S(1)}, f32[3,256,256]{2,1,0:T(8,128)S(1)}, u32[]{:S(2)}, u32[]{:S(2)}) collective-permute-start(f32[3,256,256]{2,1,0:T(8,128)S(1)} %pad_maximum_fusion), channel_id=1, source_target_pairs={{0,16},{1,17},{2,18},{3,19},{4,20},{5,21},{6,22},{7,23},{8,24},{9,... | collective-permute-start | bytes 2359304 | tf_op jit(solution)/shard_map/ppermute | solution.py:466
  29.6 1.1 broadcast_select_fusion.2
  30.7 4.1 %shard_map.28 = (f32[128,128]{1,0:T(8,128)S(1)}, f32[128,128]{1,0:T(8,128)S(1)}, f32[128,128]{1,0:T(8,128)S(1)}, f32[128,128]{1,0:T(8,128)S(1)}) custom-call(f32[3,128,128]{2,1,0:T(8,128)S(1)} %get-tuple-element.96.block), custom_call_target="tpu_custom_call" | custom-call | tf_op jit(solution)/shard_map/pallas_call | solution.py:134
  34.8 0.7 collective-permute-start.10
  35.6 1.4 fusion.1
  37.0 1.6 %collective-permute-start.5 = (f32[2,256,256]{2,1,0:T(8,128)S(1)}, f32[2,256,256]{2,1,0:T(8,128)S(1)}, u32[]{:S(2)}, u32[]{:S(2)}) collective-permute-start(f32[2,256,256]{2,1,0:T(8,128)S(1)} %get-tuple-element.66.refs_2_.refs_3_.refs_12_), channel_id=1, source_target_pairs={{0,8},{1,9},{2,10},{3,11},{4,12},{5,13},{6,14},{7,15},{8,0},{9,1},... | collective-permute-start | bytes 1572872 | tf_op jit(solution)/shard_map/ppermute | solution.py:466
  38.6 0.7 collective-permute-start.13
  39.3 1.3 collective-permute-start.8
  40.6 3.8 %shard_map.29 = (f32[256,256]{1,0:T(8,128)S(1)}, f32[256,256]{1,0:T(8,128)S(1)}) custom-call(f32[128,128]{1,0:T(8,128)S(1)} %get-tuple-element.42.factor, f32[128,128]{1,0:T(8,128)S(1)} %get-tuple-element.43.inverse, f32[128,128]{1,0:T(8,128)S(1)} %get-tuple-element.44.below, f32[128,128]{1,0:T(8,128)S(1)} %get-tuple-element.45.rest), custom_call_target="tpu_custom_call" | custom-call | tf_op jit(solution)/shard_map/pallas_call | solution.py:134
  44.4 0.7 copy-done.26
  45.1 1.8 %collective-permute-done.3 = f32[3,256,256]{2,1,0:T(8,128)S(1)} collective-permute-done((f32[3,256,256]{2,1,0:T(8,128)S(1)}, f32[3,256,256]{2,1,0:T(8,128)S(1)}, u32[]{:S(2)}, u32[]{:S(2)}) %collective-permute-start.3) | collective-permute-done | bytes 786464 | tf_op jit(solution)/shard_map/ppermute | solution.py:466
  47.1 4.1 %collective-permute-done.5.refs_4_.refs_1_.refs_14_ = f32[2,256,256]{2,1,0:T(8,128)S(1)} collective-permute-done((f32[2,256,256]{2,1,0:T(8,128)S(1)}, f32[2,256,256]{2,1,0:T(8,128)S(1)}, u32[]{:S(2)}, u32[]{:S(2)}) %collective-permute-start.5) | collective-permute-done | bytes 524320 | tf_op jit(solution)/shard_map/ppermute | solution.py:466
  51.1 1.5 %collective-permute-start.6 = (f32[3,256,256]{2,1,0:T(8,128)S(1)}, f32[3,256,256]{2,1,0:T(8,128)S(1)}, u32[]{:S(2)}, u32[]{:S(2)}) collective-permute-start(f32[3,256,256]{2,1,0:T(8,128)S(1)} %broadcast_select_fusion.refs_1_.refs_2_.refs_13_), channel_id=1, source_target_pairs={{0,8},{1,9},{2,10},{3,11},{4,12},{5,13},{6,14},{7,15},{8,0},{9,1},... | collective-permute-start | bytes 2359304 | tf_op jit(solution)/shard_map/ppermute | solution.py:466
  52.7 1.5 %collective-permute-start.9 = (f32[2,256,256]{2,1,0:T(8,128)S(1)}, f32[2,256,256]{2,1,0:T(8,128)}, u32[]{:S(2)}, u32[]{:S(2)}) collective-permute-start(f32[2,256,256]{2,1,0:T(8,128)S(1)} %slice_select_fusion), channel_id=1, source_target_pairs={{2,4},{3,5},{10,12},{11,13},{18,20},{26,21},{19,28},{27,29},{4,6},... | collective-permute-start | bytes 1572872 | tf_op jit(solution)/shard_map/ppermute | solution.py:466
  54.3 5.2 %shard_map.30 = (f32[256,256]{1,0:T(8,128)S(1)}, f32[128,128]{1,0:T(8,128)S(1)}, f32[128,128]{1,0:T(8,128)S(1)}, f32[128,128]{1,0:T(8,128)S(1)}, f32[128,128]{1,0:T(8,128)S(1)}) custom-call(f32[3,128,128]{2,1,0:T(8,128)S(1)} %get-tuple-element.41.side, f32[3,128,128]{2,1,0:T(8,128)S(1)} %get-tuple-element.74.turned, ...), custom_call_target="tpu_custom_call" | custom-call | tf_op jit(solution)/shard_map/pallas_call | solution.py:134
  59.4 1.6 %collective-permute-start.12 = (f32[3,256,256]{2,1,0:T(8,128)S(1)}, f32[3,256,256]{2,1,0:T(8,128)}, u32[]{:S(2)}, u32[]{:S(2)}) collective-permute-start(f32[3,256,256]{2,1,0:T(8,128)S(1)} %broadcast_select_fusion.refs_1_.refs_2_.refs_13_), channel_id=1, source_target_pairs={{4,2},{13,11},{22,20},{31,29}} | collective-permute-start | bytes 2359304 | tf_op jit(solution)/shard_map/ppermute | solution.py:466
  61.1 8.9 %collective-permute-done.6.refs_3_.refs_0_.refs_15_.refs_2_ = f32[3,256,256]{2,1,0:T(8,128)S(1)} collective-permute-done((f32[3,256,256]{2,1,0:T(8,128)S(1)}, f32[3,256,256]{2,1,0:T(8,128)S(1)}, u32[]{:S(2)}, u32[]{:S(2)}) %collective-permute-start.6) | collective-permute-done | bytes 786464 | tf_op jit(solution)/shard_map/ppermute | solution.py:466
  70.0 3.8 %shard_map.33 = (f32[256,256]{1,0:T(8,128)S(1)}, f32[256,256]{1,0:T(8,128)S(1)}) custom-call(f32[128,128]{1,0:T(8,128)S(1)} %get-tuple-element.53.factor, f32[128,128]{1,0:T(8,128)S(1)} %get-tuple-element.54.inverse, f32[128,128]{1,0:T(8,128)S(1)} %get-tuple-element.55.below, f32[128,128]{1,0:T(8,128)S(1)} %get-tuple-element.56.rest), custom_call_target="tpu_custom_call" | custom-call | flops 5000000000 | tf_op jit(solution)/shard_map/pallas_call | solution.py:134
  73.8 0.7 copy-done.29
  74.6 0.8 copy-done.34
  75.5 2.1 %collective-permute-start.18 = (f32[5,128,128]{2,1,0:T(8,128)S(1)}, f32[5,128,128]{2,1,0:T(8,128)}, u32[]{:S(2)}, u32[]{:S(2)}) collective-permute-start(f32[5,128,128]{2,1,0:T(8,128)S(1)} %broadcast_select_fusion.8), channel_id=1, source_target_pairs={{0,4},{1,5},{8,12},{9,13},{16,20},{17,21},{24,28},{25,29}} | collective-permute-start | bytes 983048 | tf_op jit(solution)/shard_map/ppermute | solution.py:466
  77.6 0.7 collective-permute-start.11
  78.3 1.4 collective-permute-start.15
  79.7 1.6 %collective-permute-start.14 = (f32[3,256,256]{2,1,0:T(8,128)S(1)}, f32[3,256,256]{2,1,0:T(8,128)}, u32[]{:S(2)}, u32[]{:S(2)}) collective-permute-start(f32[3,256,256]{2,1,0:T(8,128)S(1)} %collective-permute-done.6.refs_3_.refs_0_.refs_15_.refs_2_), channel_id=1, source_target_pairs={{4,3},{13,10},{22,21},{31,28}} | collective-permute-start | bytes 2359304 | tf_op jit(solution)/shard_map/ppermute | solution.py:466
  81.3 2.1 %collective-permute-done.18 = f32[5,128,128]{2,1,0:T(8,128)} collective-permute-done((f32[5,128,128]{2,1,0:T(8,128)S(1)}, f32[5,128,128]{2,1,0:T(8,128)}, u32[]{:S(2)}, u32[]{:S(2)}) %collective-permute-start.18) | collective-permute-done | bytes 327712 | tf_op jit(solution)/shard_map/ppermute | solution.py:466
  83.4 1.0 broadcast_select_fusion.4
  84.5 1.3 collective-permute-start.19
  85.8 4.5 %collective-permute-done.19 = f32[5,128,128]{2,1,0:T(8,128)S(1)} collective-permute-done((f32[5,128,128]{2,1,0:T(8,128)S(1)}, f32[5,128,128]{2,1,0:T(8,128)S(1)}, u32[]{:S(2)}, u32[]{:S(2)}) %collective-permute-start.19) | collective-permute-done | bytes 327712 | tf_op jit(solution)/shard_map/ppermute | solution.py:466
  90.4 0.8 broadcast_select_fusion.5
  91.1 6.8 %collective-permute-start.20 = (f32[5,128,128]{2,1,0:T(8,128)}, f32[5,128,128]{2,1,0:T(8,128)}, u32[]{:S(2)}, u32[]{:S(2)}) collective-permute-start(f32[5,128,128]{2,1,0:T(8,128)} %broadcast_select_fusion.5), channel_id=1, source_target_pairs={{0,1},{1,0},{2,3},{3,2},{4,5},{5,4},{6,7},{7,6},{8,9},{9,8},{10,11... | collective-permute-start | bytes 983048 | tf_op jit(solution)/shard_map/ppermute | solution.py:466
  97.9 1.0 copy-done.3
  99.1 1.8 %collective-permute-start.17 = (f32[5,256,256]{2,1,0:T(8,128)S(1)}, f32[5,256,256]{2,1,0:T(8,128)}, u32[]{:S(2)}, u32[]{:S(2)}) collective-permute-start(f32[5,256,256]{2,1,0:T(8,128)S(1)} %shard_map.32.refs_5_), channel_id=1, source_target_pairs={{4,5},{13,12},{22,23},{31,30},{18,19},{27,26}} | collective-permute-start | bytes 3932168 | tf_op jit(solution)/shard_map/ppermute | solution.py:466
  101.6 2.4 %shard_map.31.refs_3_ = f32[5,256,256]{2,1,0:T(8,128)} custom-call(s32[1]{0:T(128)} %bitcast.27.which, f32[2560,1280]{1,0:T(8,128)} %refs_1_.5, f32[3,256,256]{2,1,0:T(8,128)S(1)} %broadcast_select_fusion.refs_1_.refs_2_.refs_13_, f32[2,256,256]{2,1,0:T(8,128)S(1)} %get-tuple-element.66.refs_2_.refs_3_.refs_12_, ...), custom_call_target="tpu_custom_call" | custom-call | tf_op jit(solution)/shard_map/pallas_call | solution.py:343
  104.3 1.0 copy-done.4
  105.3 1.0 copy-done.8
  106.4 1.0 copy-done.18
  107.4 2.0 %shard_map.36.refs_3_ = f32[3,256,256]{2,1,0:T(8,128)} custom-call(s32[1]{0:T(128)} %bitcast.7.which, f32[2560,1280]{1,0:T(8,128)} %refs_1_.5, f32[3,256,256]{2,1,0:T(8,128)S(1)} %broadcast_select_fusion.refs_1_.refs_2_.refs_13_, f32[2,256,256]{2,1,0:T(8,128)S(1)} %get-tuple-element.66.refs_2_.refs_3_.refs_12_, ...), custom_call_target="tpu_custom_call" | custom-call | tf_op jit(solution)/shard_map/pallas_call | solution.py:343
  109.5 0.5 collective-permute-start.22
  110.0 1.1 broadcast_select_fusion.6
  111.4 0.9 copy-done.5
  112.6 13.6 %shard_map.34 = (f32[2560,1280]{1,0:T(8,128)}, bf16[512,1280]{1,0:T(8,128)(2,1)S(1)}, bf16[512,1280]{1,0:T(8,128)(2,1)S(1)}) custom-call(s32[7]{0:T(128)S(1)} %stack.134.refs_0_, f32[2560,1280]{1,0:T(8,128)} %refs_1_.5, f32[10,1,256]{2,1,0:T(1,128)S(1)} %reshape.21.refs_2_, f32[5,256,256]{2,1,0:T(8,128)} %shard_map.31.refs_3_, ...), custom_call_target="tpu_custom_call" | custom-call | flops 5536481280 | bytes 13107200 | tf_op jit(solution)/shard_map/pallas_call | solution.py:291
  126.3 1.1 copy-done.13
  127.4 2.4 %shard_map.35.refs_3_ = f32[2,256,256]{2,1,0:T(8,128)} custom-call(s32[1]{0:T(128)} %bitcast.7.which, f32[2560,1280]{1,0:T(8,128)} %refs_1_.5, f32[3,256,256]{2,1,0:T(8,128)S(1)} %broadcast_select_fusion.refs_1_.refs_2_.refs_13_, f32[3,256,256]{2,1,0:T(8,128)S(1)} %collective-permute-done.6.refs_3_.refs_0_.refs_15_.refs_2_, f32[2,256,256]{2,1,0:T(8,128)S(1)} %copy-done.9, ...), custom_call_target="tpu_custom_call" | custom-call | tf_op jit(solution)/shard_map/pallas_call | solution.py:343
  130.0 1.3 copy-done.11
  131.4 1.3 copy-done.14
  132.7 0.9 copy-done.24
  133.6 0.9 copy-done.28
  134.6 0.9 copy-done.31
  135.5 6.7 %shard_map.37.refs_14_ = f32[2560,1280]{1,0:T(8,128)} custom-call(s32[7]{0:T(128)S(1)} %stack.122.refs_0_, f32[2560,1280]{1,0:T(8,128)} %refs_1_.5, f32[10,1,256]{2,1,0:T(1,128)S(1)} %reshape.21.refs_2_, f32[3,256,256]{2,1,0:T(8,128)} %shard_map.36.refs_3_, f32[3,256,256]{2,1,0:T(8,128)} %collective-permute-done.22.refs_4_, ...), custom_call_target="tpu_custom_call", output_to_operand_aliasing={{}: (14, {})} | custom-call | flops 2415919104 | bytes 7864320 | tf_op jit(solution)/shard_map/pallas_call | solution.py:291
  142.3 6.2 %shard_map.38 = f32[2560,1280]{1,0:T(8,128)} custom-call(s32[7]{0:T(128)S(1)} %stack.122.refs_0_, f32[2560,1280]{1,0:T(8,128)} %refs_1_.5, f32[10,1,256]{2,1,0:T(1,128)S(1)} %reshape.21.refs_2_, f32[2,256,256]{2,1,0:T(8,128)} %shard_map.35.refs_3_, f32[2,256,256]{2,1,0:T(8,128)S(1)} %collective-permute-done.21.refs_4_, ...), custom_call_target="tpu_custom_call", output_to_operand_aliasing={{}: (14, {})} | custom-call | flops 1610612736 | bytes 5242880 | tf_op jit(solution)/shard_map/pallas_call | solution.py:291
  (115 shorter events, 2.2 us)
Async XLA Ops:
  1.8 5.0 %slice-start = ((f32[2560,1280]{1,0:T(8,128)}), f32[256,1280]{1,0:T(8,128)S(1)}, s32[]{:S(2)}) async-start(f32[2560,1280]{1,0:T(8,128)} %refs_1_.5), calls=%async_computation | async-start | bytes 2621440 | tf_op jit(solution)/shard_map/slice | solution.py:519
  1.8 9.9 %collective-permute-start = (f32[3,128,128]{2,1,0:T(8,128)S(1)}, f32[3,128,128]{2,1,0:T(8,128)S(1)}, u32[]{:S(2)}, u32[]{:S(2)}) collective-permute-start(f32[3,128,128]{2,1,0:T(8,128)S(1)} %pad_maximum_fusion.2), channel_id=1, source_target_pairs={{0,16},{1,17},{8,24},{9,25}} | collective-permute-start | bytes 589832 | tf_op jit(solution)/shard_map/ppermute | solution.py:466
  9.6 25.2 %collective-permute-start.4 = (f32[2,256,256]{2,1,0:T(8,128)S(1)}, f32[2,256,256]{2,1,0:T(8,128)}, u32[]{:S(2)}, u32[]{:S(2)}) collective-permute-start(f32[2,256,256]{2,1,0:T(8,128)S(1)} %bitcast.97), channel_id=1, source_target_pairs={{0,16},{1,17},{2,18},{3,19},{4,20},{5,21},{6,22},{7,23},{8,24},{9,... | collective-permute-start | bytes 1572872 | tf_op jit(solution)/shard_map/ppermute | solution.py:466
  11.7 8.3 %collective-permute-start.1 = (f32[3,128,128]{2,1,0:T(8,128)S(1)}, f32[3,128,128]{2,1,0:T(8,128)S(1)}, u32[]{:S(2)}, u32[]{:S(2)}) collective-permute-start(f32[3,128,128]{2,1,0:T(8,128)S(1)} %broadcast_select_fusion.9), channel_id=1, source_target_pairs={{0,8},{1,9},{8,0},{9,1},{16,24},{17,25},{24,16},{25,17}} | collective-permute-start | bytes 589832 | tf_op jit(solution)/shard_map/ppermute | solution.py:466
  17.0 18.6 %collective-permute-start.7 = (f32[2,256,256]{2,1,0:T(8,128)}, f32[2,256,256]{2,1,0:T(8,128)S(1)}, u32[]{:S(2)}, u32[]{:S(2)}) collective-permute-start(f32[2,256,256]{2,1,0:T(8,128)} %fusion), channel_id=1, source_target_pairs={{0,2},{1,3},{8,10},{9,11},{4,6},{12,7},{5,14},{13,15}} | collective-permute-start | bytes 1572872 | tf_op jit(solution)/shard_map/ppermute | solution.py:466
  20.8 5.6 %collective-permute-start.2 = (f32[2,3,128,128]{3,2,1,0:T(8,128)}, f32[2,3,128,128]{3,2,1,0:T(8,128)}, u32[]{:S(2)}, u32[]{:S(2)}) collective-permute-start(f32[2,3,128,128]{3,2,1,0:T(8,128)} %pad_maximum_fusion.1), channel_id=1, source_target_pairs={{0,1},{1,0},{8,9},{9,8},{16,17},{17,16},{24,25},{25,24}} | collective-permute-start | bytes 1179656 | tf_op jit(solution)/shard_map/ppermute | solution.py:466
  26.3 8.5 %copy-start.39 = (f32[5,256,256]{2,1,0:T(8,128)S(1)}, f32[5,256,256]{2,1,0:T(8,128)}, u32[]{:S(2)}) copy-start(f32[5,256,256]{2,1,0:T(8,128)} %slice_bitcast_fusion) | copy-start | bytes 3932164
  26.3 20.7 %collective-permute-start.3 = (f32[3,256,256]{2,1,0:T(8,128)S(1)}, f32[3,256,256]{2,1,0:T(8,128)S(1)}, u32[]{:S(2)}, u32[]{:S(2)}) collective-permute-start(f32[3,256,256]{2,1,0:T(8,128)S(1)} %pad_maximum_fusion), channel_id=1, source_target_pairs={{0,16},{1,17},{2,18},{3,19},{4,20},{5,21},{6,22},{7,23},{8,24},{9,... | collective-permute-start | bytes 2359304 | tf_op jit(solution)/shard_map/ppermute | solution.py:466
  34.8 19.4 %collective-permute-start.10 = (f32[5,256,256]{2,1,0:T(8,128)S(1)}, f32[5,256,256]{2,1,0:T(8,128)S(1)}, u32[]{:S(2)}, u32[]{:S(2)}) collective-permute-start(f32[5,256,256]{2,1,0:T(8,128)S(1)} %copy-done.39), channel_id=1, source_target_pairs={{16,18},{17,19},{24,26},{25,27}} | collective-permute-start | bytes 3932168 | tf_op jit(solution)/shard_map/ppermute | solution.py:466
  35.6 1.4 copy-start.16
  37.0 14.1 %collective-permute-start.5 = (f32[2,256,256]{2,1,0:T(8,128)S(1)}, f32[2,256,256]{2,1,0:T(8,128)S(1)}, u32[]{:S(2)}, u32[]{:S(2)}) collective-permute-start(f32[2,256,256]{2,1,0:T(8,128)S(1)} %get-tuple-element.66.refs_2_.refs_3_.refs_12_), channel_id=1, source_target_pairs={{0,8},{1,9},{2,10},{3,11},{4,12},{5,13},{6,14},{7,15},{8,0},{9,1},... | collective-permute-start | bytes 1572872 | tf_op jit(solution)/shard_map/ppermute | solution.py:466
  38.6 36.0 %collective-permute-start.13 = (f32[2,256,256]{2,1,0:T(8,128)S(1)}, f32[2,256,256]{2,1,0:T(8,128)S(1)}, u32[]{:S(2)}, u32[]{:S(2)}) collective-permute-start(f32[2,256,256]{2,1,0:T(8,128)S(1)} %get-tuple-element.66.refs_2_.refs_3_.refs_12_), channel_id=1, source_target_pairs={{4,2},{13,11},{22,20},{31,29}} | collective-permute-start | bytes 1572872 | tf_op jit(solution)/shard_map/ppermute | solution.py:466
  39.3 13.4 %collective-permute-start.8 = (f32[2,256,256]{2,1,0:T(8,128)S(1)}, f32[2,256,256]{2,1,0:T(8,128)S(1)}, u32[]{:S(2)}, u32[]{:S(2)}) collective-permute-start(f32[2,256,256]{2,1,0:T(8,128)S(1)} %get-tuple-element.65), channel_id=1, source_target_pairs={{0,2},{1,3},{8,10},{9,11},{2,4},{3,5},{10,12},{11,13},{18,20},{26,... | collective-permute-start | bytes 1572872 | tf_op jit(solution)/shard_map/ppermute | solution.py:466
  51.1 27.1 %copy-start.2 = (f32[2,256,256]{2,1,0:T(8,128)}, f32[2,256,256]{2,1,0:T(8,128)S(1)}, u32[]{:S(2)}) copy-start(f32[2,256,256]{2,1,0:T(8,128)S(1)} %collective-permute-done.5.refs_4_.refs_1_.refs_14_) | copy-start | bytes 1572868
  51.1 18.8 %collective-permute-start.6 = (f32[3,256,256]{2,1,0:T(8,128)S(1)}, f32[3,256,256]{2,1,0:T(8,128)S(1)}, u32[]{:S(2)}, u32[]{:S(2)}) collective-permute-start(f32[3,256,256]{2,1,0:T(8,128)S(1)} %broadcast_select_fusion.refs_1_.refs_2_.refs_13_), channel_id=1, source_target_pairs={{0,8},{1,9},{2,10},{3,11},{4,12},{5,13},{6,14},{7,15},{8,0},{9,1},... | collective-permute-start | bytes 2359304 | tf_op jit(solution)/shard_map/ppermute | solution.py:466
  52.6 8.4 %copy-start.6 = (f32[2,256,256]{2,1,0:T(8,128)}, f32[2,256,256]{2,1,0:T(8,128)S(1)}, u32[]{:S(2)}) copy-start(f32[2,256,256]{2,1,0:T(8,128)S(1)} %collective-permute-done.8.refs_7_.refs_3_.refs_6_) | copy-start | bytes 1572868
  52.7 22.7 %collective-permute-start.9 = (f32[2,256,256]{2,1,0:T(8,128)S(1)}, f32[2,256,256]{2,1,0:T(8,128)}, u32[]{:S(2)}, u32[]{:S(2)}) collective-permute-start(f32[2,256,256]{2,1,0:T(8,128)S(1)} %slice_select_fusion), channel_id=1, source_target_pairs={{2,4},{3,5},{10,12},{11,13},{18,20},{26,21},{19,28},{27,29},{4,6},... | collective-permute-start | bytes 1572872 | tf_op jit(solution)/shard_map/ppermute | solution.py:466
  54.3 19.5 %copy-start.32 = (f32[5,256,256]{2,1,0:T(8,128)}, f32[5,256,256]{2,1,0:T(8,128)S(1)}, u32[]{:S(2)}) copy-start(f32[5,256,256]{2,1,0:T(8,128)S(1)} %collective-permute-done.10.refs_5_) | copy-start | bytes 3932164
  59.4 25.0 %collective-permute-start.12 = (f32[3,256,256]{2,1,0:T(8,128)S(1)}, f32[3,256,256]{2,1,0:T(8,128)}, u32[]{:S(2)}, u32[]{:S(2)}) collective-permute-start(f32[3,256,256]{2,1,0:T(8,128)S(1)} %broadcast_select_fusion.refs_1_.refs_2_.refs_13_), channel_id=1, source_target_pairs={{4,2},{13,11},{22,20},{31,29}} | collective-permute-start | bytes 2359304 | tf_op jit(solution)/shard_map/ppermute | solution.py:466
  73.8 0.7 copy-start.29
  74.6 6.7 %copy-start.38 = (f32[5,128,128]{2,1,0:T(8,128)}, f32[5,128,128]{2,1,0:T(8,128)S(1)}, u32[]{:S(2)}) copy-start(f32[5,128,128]{2,1,0:T(8,128)S(1)} %broadcast_select_fusion.8) | copy-start | bytes 983044
  74.6 0.8 copy-start.34
  75.5 8.0 %collective-permute-start.18 = (f32[5,128,128]{2,1,0:T(8,128)S(1)}, f32[5,128,128]{2,1,0:T(8,128)}, u32[]{:S(2)}, u32[]{:S(2)}) collective-permute-start(f32[5,128,128]{2,1,0:T(8,128)S(1)} %broadcast_select_fusion.8), channel_id=1, source_target_pairs={{0,4},{1,5},{8,12},{9,13},{16,20},{17,21},{24,28},{25,29}} | collective-permute-start | bytes 983048 | tf_op jit(solution)/shard_map/ppermute | solution.py:466
  77.6 6.9 %collective-permute-start.11 = (f32[2,256,256]{2,1,0:T(8,128)}, f32[2,256,256]{2,1,0:T(8,128)S(1)}, u32[]{:S(2)}, u32[]{:S(2)}) collective-permute-start(f32[2,256,256]{2,1,0:T(8,128)} %collective-permute-done.9.refs_4_.refs_7_), channel_id=1, source_target_pairs={{4,6},{5,7},{12,14},{13,15},{20,22},{21,23},{28,30},{29,31}} | collective-permute-start | bytes 1572872 | tf_op jit(solution)/shard_map/ppermute | solution.py:466
  78.3 6.2 %collective-permute-start.15 = (f32[2,256,256]{2,1,0:T(8,128)S(1)}, f32[2,256,256]{2,1,0:T(8,128)}, u32[]{:S(2)}, u32[]{:S(2)}) collective-permute-start(f32[2,256,256]{2,1,0:T(8,128)S(1)} %collective-permute-done.5.refs_4_.refs_1_.refs_14_), channel_id=1, source_target_pairs={{4,3},{13,10},{22,21},{31,28}} | collective-permute-start | bytes 1572872 | tf_op jit(solution)/shard_map/ppermute | solution.py:466
  79.7 21.3 %collective-permute-start.14 = (f32[3,256,256]{2,1,0:T(8,128)S(1)}, f32[3,256,256]{2,1,0:T(8,128)}, u32[]{:S(2)}, u32[]{:S(2)}) collective-permute-start(f32[3,256,256]{2,1,0:T(8,128)S(1)} %collective-permute-done.6.refs_3_.refs_0_.refs_15_.refs_2_), channel_id=1, source_target_pairs={{4,3},{13,10},{22,21},{31,28}} | collective-permute-start | bytes 2359304 | tf_op jit(solution)/shard_map/ppermute | solution.py:466
  84.4 13.5 %copy-start.36 = (f32[2,256,256]{2,1,0:T(8,128)}, f32[2,256,256]{2,1,0:T(8,128)S(1)}, u32[]{:S(2)}) copy-start(f32[2,256,256]{2,1,0:T(8,128)S(1)} %collective-permute-done.11.refs_5_) | copy-start | bytes 1572868
  84.5 5.9 %collective-permute-start.19 = (f32[5,128,128]{2,1,0:T(8,128)S(1)}, f32[5,128,128]{2,1,0:T(8,128)S(1)}, u32[]{:S(2)}, u32[]{:S(2)}) collective-permute-start(f32[5,128,128]{2,1,0:T(8,128)S(1)} %broadcast_select_fusion.4), channel_id=1, source_target_pairs={{0,2},{1,3},{4,6},{5,7},{8,10},{9,11},{12,14},{13,15},{16,18},{17,... | collective-permute-start | bytes 983048 | tf_op jit(solution)/shard_map/ppermute | solution.py:466
  91.1 18.9 %collective-permute-start.20 = (f32[5,128,128]{2,1,0:T(8,128)}, f32[5,128,128]{2,1,0:T(8,128)}, u32[]{:S(2)}, u32[]{:S(2)}) collective-permute-start(f32[5,128,128]{2,1,0:T(8,128)} %broadcast_select_fusion.5), channel_id=1, source_target_pairs={{0,1},{1,0},{2,3},{3,2},{4,5},{5,4},{6,7},{7,6},{8,9},{9,8},{10,11... | collective-permute-start | bytes 983048 | tf_op jit(solution)/shard_map/ppermute | solution.py:466
  97.9 1.0 copy-start.3
  99.0 2.0 %copy-start.7 = (f32[2,256,256]{2,1,0:T(8,128)S(1)}, f32[2,256,256]{2,1,0:T(8,128)}, u32[]{:S(2)}) copy-start(f32[2,256,256]{2,1,0:T(8,128)} %copy-done.6) | copy-start | bytes 1572868
  99.0 2.0 %copy-start.17 = (f32[2,256,256]{2,1,0:T(8,128)S(1)}, f32[2,256,256]{2,1,0:T(8,128)}, u32[]{:S(2)}) copy-start(f32[2,256,256]{2,1,0:T(8,128)} %copy-done.16) | copy-start | bytes 1572868
  99.0 2.6 %copy-start.33 = (f32[5,256,256]{2,1,0:T(8,128)S(1)}, f32[5,256,256]{2,1,0:T(8,128)}, u32[]{:S(2)}) copy-start(f32[5,256,256]{2,1,0:T(8,128)} %copy-done.32) | copy-start | bytes 3932164
  99.0 2.7 %copy-start.35 = (f32[2,256,256]{2,1,0:T(8,128)S(1)}, f32[2,256,256]{2,1,0:T(8,128)}, u32[]{:S(2)}) copy-start(f32[2,256,256]{2,1,0:T(8,128)} %copy-done.34) | copy-start | bytes 1572868
  99.1 4.9 %copy-start = (f32[5,256,256]{2,1,0:T(8,128)}, f32[5,256,256]{2,1,0:T(8,128)S(1)}, u32[]{:S(2)}) copy-start(f32[5,256,256]{2,1,0:T(8,128)S(1)} %shard_map.32.refs_5_) | copy-start | bytes 3932164
  99.1 12.2 %collective-permute-start.17 = (f32[5,256,256]{2,1,0:T(8,128)S(1)}, f32[5,256,256]{2,1,0:T(8,128)}, u32[]{:S(2)}, u32[]{:S(2)}) collective-permute-start(f32[5,256,256]{2,1,0:T(8,128)S(1)} %shard_map.32.refs_5_), channel_id=1, source_target_pairs={{4,5},{13,12},{22,23},{31,30},{18,19},{27,26}} | collective-permute-start | bytes 3932168 | tf_op jit(solution)/shard_map/ppermute | solution.py:466
  101.6 2.5 %copy-start.40 = (f32[2560]{0:T(1024)S(1)}, f32[2560]{0:T(1024)}, u32[]{:S(2)}) copy-start(f32[2560]{0:T(1024)} %param.3) | copy-start | bytes 30724
  104.1 7.3 %collective-permute-start.16 = (f32[5,256,256]{2,1,0:T(8,128)}, f32[5,256,256]{2,1,0:T(8,128)}, u32[]{:S(2)}, u32[]{:S(2)}) collective-permute-start(f32[5,256,256]{2,1,0:T(8,128)} %shard_map.31.refs_3_), channel_id=1, source_target_pairs={{0,1},{1,0},{2,3},{3,2},{4,5},{5,4},{6,7},{7,6},{8,9},{9,8},{10,11... | collective-permute-start | bytes 3932168 | tf_op jit(solution)/shard_map/ppermute | solution.py:466
  104.3 1.0 copy-start.4
  105.3 1.0 copy-start.8
  106.4 1.0 copy-start.18
  109.5 20.5 %collective-permute-start.22 = (f32[3,256,256]{2,1,0:T(8,128)}, f32[3,256,256]{2,1,0:T(8,128)}, u32[]{:S(2)}, u32[]{:S(2)}) collective-permute-start(f32[3,256,256]{2,1,0:T(8,128)} %shard_map.36.refs_3_), channel_id=1, source_target_pairs={{0,1},{1,0},{2,3},{3,2},{4,5},{5,4},{6,7},{7,6},{8,9},{9,8},{10,11... | collective-permute-start | bytes 2359304 | tf_op jit(solution)/shard_map/ppermute | solution.py:466
  111.2 1.2 copy-start.5
  111.2 1.4 copy-start.27
  111.2 1.5 copy-start.30
  111.3 15.0 %copy-start.19 = (f32[256,256]{1,0:T(8,128)}, f32[256,256]{1,0:T(8,128)S(1)}, u32[]{:S(2)}) copy-start(f32[256,256]{1,0:T(8,128)S(1)} %select_maximum_fusion.1.refs_8_) | copy-start | bytes 786436
  111.3 15.0 %copy-start.21 = (f32[256,256]{1,0:T(8,128)}, f32[256,256]{1,0:T(8,128)S(1)}, u32[]{:S(2)}) copy-start(f32[256,256]{1,0:T(8,128)S(1)} %select_maximum_fusion.refs_11_) | copy-start | bytes 786436
  111.4 14.9 %copy-start.23 = (f32[256,256]{1,0:T(8,128)}, f32[256,256]{1,0:T(8,128)S(1)}, u32[]{:S(2)}) copy-start(f32[256,256]{1,0:T(8,128)S(1)} %maximum_maximum_fusion.refs_9_) | copy-start | bytes 786436
  112.6 14.8 %copy-start.9 = (f32[2,256,256]{2,1,0:T(8,128)S(1)}, f32[2,256,256]{2,1,0:T(8,128)}, u32[]{:S(2)}) copy-start(f32[2,256,256]{2,1,0:T(8,128)} %copy-done.6) | copy-start | bytes 1572868
  112.6 14.8 %copy-start.37 = (f32[2,256,256]{2,1,0:T(8,128)S(1)}, f32[2,256,256]{2,1,0:T(8,128)}, u32[]{:S(2)}) copy-start(f32[2,256,256]{2,1,0:T(8,128)} %copy-done.36) | copy-start | bytes 1572868
  126.3 1.1 copy-start.13
  127.4 2.4 %copy-start.10 = (bf16[512,1280]{1,0:T(8,128)(2,1)}, bf16[512,1280]{1,0:T(8,128)(2,1)S(1)}, u32[]{:S(2)}) copy-start(bf16[512,1280]{1,0:T(8,128)(2,1)S(1)} %get-tuple-element.61.refs_12_) | copy-start | bytes 3932164
  127.4 2.6 %copy-start.1 = (f32[5,256,256]{2,1,0:T(8,128)S(1)}, f32[5,256,256]{2,1,0:T(8,128)}, u32[]{:S(2)}) copy-start(f32[5,256,256]{2,1,0:T(8,128)} %copy-done) | copy-start | bytes 3932164
  127.4 2.6 %copy-start.20 = (f32[256,256]{1,0:T(8,128)S(1)}, f32[256,256]{1,0:T(8,128)}, u32[]{:S(2)}) copy-start(f32[256,256]{1,0:T(8,128)} %copy-done.19) | copy-start | bytes 786436
  127.4 2.6 %copy-start.22 = (f32[256,256]{1,0:T(8,128)S(1)}, f32[256,256]{1,0:T(8,128)}, u32[]{:S(2)}) copy-start(f32[256,256]{1,0:T(8,128)} %copy-done.21) | copy-start | bytes 786436
  129.8 12.4 %collective-permute-start.21 = (f32[2,256,256]{2,1,0:T(8,128)}, f32[2,256,256]{2,1,0:T(8,128)S(1)}, u32[]{:S(2)}, u32[]{:S(2)}) collective-permute-start(f32[2,256,256]{2,1,0:T(8,128)} %shard_map.35.refs_3_), channel_id=1, source_target_pairs={{0,1},{1,0},{2,3},{3,2},{4,5},{5,4},{6,7},{7,6},{8,9},{9,8},{10,11... | collective-permute-start | bytes 1572872 | tf_op jit(solution)/shard_map/ppermute | solution.py:466
  130.0 1.3 copy-start.11
  131.4 1.3 copy-start.14
  132.7 0.9 copy-start.24
  133.6 0.9 copy-start.28
  134.6 0.9 copy-start.31
  135.5 6.7 %copy-start.12 = (bf16[512,1280]{1,0:T(8,128)(2,1)S(1)}, bf16[512,1280]{1,0:T(8,128)(2,1)}, u32[]{:S(2)}) copy-start(bf16[512,1280]{1,0:T(8,128)(2,1)} %copy-done.10) | copy-start | bytes 3932164
  135.5 6.7 %copy-start.15 = (bf16[512,1280]{1,0:T(8,128)(2,1)S(1)}, bf16[512,1280]{1,0:T(8,128)(2,1)}, u32[]{:S(2)}) copy-start(bf16[512,1280]{1,0:T(8,128)(2,1)} %copy-done.13) | copy-start | bytes 3932164
  135.5 6.8 %copy-start.25 = (f32[256,256]{1,0:T(8,128)S(1)}, f32[256,256]{1,0:T(8,128)}, u32[]{:S(2)}) copy-start(f32[256,256]{1,0:T(8,128)} %copy-done.23) | copy-start | bytes 786436
  (1 other events, 0.7 us)
